TPU v7x, 32 devices: a whole 2x2x4 slice. The times are simulated.
32 devices in a mesh: orb: 8 (over z, x), grp: 4 (over y, core).
Axes of the slice: x: 2, y: 2, z: 4, core: 2. Of those that a mesh axis runs over, the one named last changes fastest.
Arguments:
- orbitals: float32 [64, 48, 2304], P(('orb', 'grp')), may hold values from -6 to 6
- kernel: float32 [48, 2304], replicated, may hold values from 0.1 to 2
- anchors: int32 [8, 3], replicated, may hold values from 0 to 16
- pair_count: int32 [8], P('orb'), may hold values from 1 to 8, 32 in all
- pair_first: int32 [64], P('orb'), may hold values from 0 to 7
- pair_second: int32 [64], P('orb'), may hold values from 0 to 7
- pair_reach: int32 [64], P('orb'), may hold values from 0 to 2
Outputs:
- gradient: float32 [64, 48, 2304], P('orb', 'grp')
- lagrange: float32 [8, 8, 8], P('orb')
Inputs may be any that keep to these rules, and one draw needn't show every extreme that they name: The live slots of a fragment are its first pair_count slots; some fragment has all 8 live.
All inputs are finite; a program needn't handle non-finite values. No bound on the sum of `pair_count` on one device may be relied on, other than what follows from the above.
Results may differ from a plain program's by a relative error of at most 0.0003.
Values sent between devices are 32-bit elements; how exact they have to be, the bound alone decides.
No kernel may reach another device: no remote copies, remote signals or barrier semaphores. Data moves between devices by JAX's collectives and lax.ppermute only.
A program may use at most 128 MiB of HBM per device.

v0:
```python
import functools
import math

import jax
import jax.numpy as jnp
import numpy as np
from jax import lax
from jax.experimental import pallas as pl
from jax.experimental.pallas import tpu as pltpu
from jax.sharding import PartitionSpec as P

REACH = 2
LANES = 128
ROWS = 8
HALF = LANES // 2


class Number:
    def __init__(self, real, imag=None):
        self.real, self.imag = real, imag

    def __add__(self, other):
        if self.imag is None or other.imag is None:
            imag = self.imag if other.imag is None else other.imag
        else:
            imag = self.imag + other.imag
        return Number(self.real + other.real, imag)

    def __sub__(self, other):
        if other.imag is None:
            imag = self.imag
        else:
            imag = -other.imag if self.imag is None else self.imag - other.imag
        return Number(self.real - other.real, imag)

    def conj(self):
        return self if self.imag is None else Number(self.real, -self.imag)

    def scaled(self, factor):
        return Number(self.real * factor, None if self.imag is None else self.imag * factor)

    def turned(self, sign):
        if self.imag is None:
            return Number(jnp.zeros_like(self.real), self.real if sign > 0 else -self.real)
        return Number(-self.imag, self.real) if sign > 0 else Number(self.imag, -self.real)

    def plus_turned(self, other, sign):
        if sign < 0:
            return self.minus_turned(other)
        real = self.real if other.imag is None else self.real - other.imag
        return Number(real, other.real if self.imag is None else self.imag + other.real)

    def minus_turned(self, other):
        real = self.real if other.imag is None else self.real + other.imag
        return Number(real, -other.real if self.imag is None else self.imag - other.real)

    def times(self, angle):
        real, imag = math.cos(angle), math.sin(angle)
        if abs(imag) < 1e-12:
            return self if real > 0 else self.scaled(-1.0)
        if abs(real) < 1e-12:
            return self.turned(imag)
        if self.imag is None:
            return Number(self.real * real, self.real * imag)
        return Number(self.real * real - self.imag * imag, self.real * imag + self.imag * real)


def coprime(n):
    for p in (2, 3, 5, 7):
        power = 1
        while n % (power * p) == 0:
            power *= p
        if 1 < power < n:
            return power, n // power
    return None


def radix(n):
    return next((p for p in (4, 2, 3, 5, 7) if n % p == 0 and n > p), None)


def meeting(i, j, first, second):
    return next(k for k in range(first * second) if k % first == i and k % second == j)


def dft(values, sign):
    n = len(values)
    if n == 1:
        return values
    if n == 2:
        return [values[0] + values[1], values[0] - values[1]]
    if n == 3:
        a, b, c = values
        total, side = b + c, (b - c).scaled(math.sqrt(0.75))
        middle = a - total.scaled(0.5)
        return [a + total, middle.plus_turned(side, sign), middle.plus_turned(side, -sign)]
    if n == 4:
        a, b, c, d = values
        s, t, u, v = a + c, a - c, b + d, b - d
        return [s + u, t.plus_turned(v, sign), s - u, t.plus_turned(v, -sign)]
    out = [None] * n
    if coprime(n):
        first, second = coprime(n)
        columns = [
            dft([values[(i * second + j * first) % n] for i in range(first)], sign)
            for j in range(second)
        ]
        for i in range(first):
            row = dft([column[i] for column in columns], sign)
            for j in range(second):
                out[meeting(i, j, first, second)] = row[j]
        return out
    p = radix(n)
    if p:
        rest = n // p
        columns = [dft(values[j::p], sign) for j in range(p)]
        for i in range(rest):
            row = dft(
                [columns[j][i].times(sign * 2.0 * math.pi * i * j / n) for j in range(p)], sign
            )
            for j in range(p):
                out[i + rest * j] = row[j]
        return out
    for k in range(n):
        total = values[0]
        for j in range(1, n):
            total = total + values[j].times(sign * 2.0 * math.pi * (j * k % n) / n)
        out[k] = total
    return out


def real_dft(values):
    n = len(values)
    if n <= 4:
        out = dft(values, -1)
    else:
        out = [None] * n
        if coprime(n):
            first, second = coprime(n)
            columns = [
                real_dft([values[(i * second + j * first) % n] for i in range(first)])
                for j in range(second)
            ]
            for i in range(first // 2 + 1):
                entries = [column[i] for column in columns]
                alone = 2 * i % first == 0
                row = real_dft(entries) if alone else dft(entries, -1)
                for j in range(second):
                    out[meeting(i, j, first, second)] = row[j]
        elif radix(n):
            p = radix(n)
            rest = n // p
            columns = [real_dft(values[j::p]) for j in range(p)]
            for i in range(rest // 2 + 1):
                row = dft(
                    [columns[j][i].times(-2.0 * math.pi * i * j / n) for j in range(p)], -1
                )
                for j in range(p):
                    out[i + rest * j] = row[j]
        else:
            out = dft(values, -1)
    for k in range(1, n):
        if out[k] is None or (k > n // 2 and out[n - k] is not None):
            out[k] = out[n - k].conj()
    out[0] = Number(out[0].real)
    if n % 2 == 0:
        out[n // 2] = Number(out[n // 2].real)
    return out


def real_back(values):
    n = len(values)
    if n == 1:
        return [values[0].real]
    if n == 2:
        return [values[0].real + values[1].real, values[0].real - values[1].real]
    if n == 3:
        a, b = values[0].real, values[1]
        side = b.imag * math.sqrt(3.0)
        middle = a - b.real
        return [a + 2.0 * b.real, middle - side, middle + side]
    if n == 4:
        s, t = values[0].real + values[2].real, values[0].real - values[2].real
        u, v = 2.0 * values[1].real, 2.0 * values[1].imag
        return [s + u, t - v, s - u, t + v]
    out = [None] * n
    if coprime(n):
        first, second = coprime(n)
        rows = []
        for i in range(first // 2 + 1):
            entries = [values[meeting(i, j, first, second)] for j in range(second)]
            if 2 * i % first == 0:
                rows.append([Number(value) for value in real_back(entries)])
            else:
                rows.append(dft(entries, 1))
        for b in range(second):
            half = [row[b] for row in rows]
            whole = half + [half[first - i].conj() for i in range(len(half), first)]
            for a, value in enumerate(real_back(whole)):
                out[(a * second + b * first) % n] = value
        return out
    p = radix(n)
    if p:
        rest = n // p
        parts = []
        for i in range(p // 2 + 1):
            entries = values[i::p]
            if i == 0:
                parts.append([Number(value) for value in real_back(entries)])
            else:
                inner = dft(entries, 1)
                parts.append([inner[m].times(2.0 * math.pi * i * m / n) for m in range(rest)])
                if 2 * i == p:
                    parts[-1] = [Number(value.real) for value in parts[-1]]
        for m in range(rest):
            half = [part[m] for part in parts]
            whole = half + [half[p - i].conj() for i in range(len(half), p)]
            for j, value in enumerate(real_back(whole)):
                out[m + rest * j] = value
        return out
    return [value.real for value in dft(values, 1)]


def wave_table(edge):
    index = np.arange(edge)
    angles = 2.0 * np.pi / edge * (np.outer(index, index) % edge)
    full = np.zeros((2, 2, HALF, 2, HALF))
    for side in range(2):
        full[0, side, :edge, side, :edge] = np.cos(angles)
        full[1, side, :edge, side, :edge] = np.sin(angles)
    full = full.reshape(2, LANES, LANES)
    high = full.astype(jnp.bfloat16)
    low = (full - high.astype(np.float64)).astype(jnp.bfloat16)
    return np.stack([high, low])


def split_dot(real, imag, matrix):
    value = jnp.concatenate([real, imag], axis=1)
    high = value.astype(jnp.bfloat16)
    low = (value - high.astype(jnp.float32)).astype(jnp.bfloat16)
    product = jnp.dot(
        jnp.concatenate([high, low, high], axis=1), matrix[...], preferred_element_type=jnp.float32
    )
    return product[:, :LANES], product[:, LANES:]


def padded_half(edge):
    return -(-(edge // 2 + 1) // ROWS) * ROWS


def screen_kernel(edge, numbers_ref, kernel_ref, waves_ref, out_ref, kept_ref, ahead_ref, behind_ref, flipped):
    for i in range(numbers_ref.shape[0]):
        kept_ref[i] = numbers_ref[i]
    for table, sign in ((ahead_ref, -1), (behind_ref, 1)):
        for part, source in enumerate((0, 0, 1)):
            for i in range(2):
                for j in range(2):
                    value = waves_ref[source, (i + j) % 2]
                    if i != j and (i > j) == (sign > 0):
                        value = -value
                    rows = slice((2 * part + i) * LANES, (2 * part + i + 1) * LANES)
                    table[rows, j * LANES : (j + 1) * LANES] = value
    exact = dict(precision=lax.Precision.HIGHEST, preferred_element_type=jnp.float32)

    def index(shape, axis):
        return lax.broadcasted_iota(jnp.int32, shape, axis)

    square, whole = (edge, edge), (LANES, LANES)
    flip = index(square, 0) + index(square, 1)
    flip = ((flip == 0) | (flip == edge)).astype(jnp.float32)
    source, target = index(whole, 0), index(whole, 1)
    target = jnp.where(target < HALF, target, target - HALF)
    mirror = ((source + target == 0) | (source + target == edge)) & (source < edge) & (target < edge)
    mirror = mirror.astype(jnp.float32)
    flipped[...] = jnp.dot(flip, kernel_ref[...], **exact)
    height = padded_half(edge)
    lane = index((edge, LANES), 1)
    out_ref[...] = jnp.zeros_like(out_ref)

    def piece(ref, y):
        begin, offset = divmod(y * edge, LANES)
        value = ref[:, begin * LANES : (begin + 1) * LANES]
        value = pltpu.roll(value, LANES - offset, 1) if offset else value
        if offset + edge > LANES:
            more = ref[:, (begin + 1) * LANES : (begin + 2) * LANES]
            value = jnp.where(lane < LANES - offset, value, pltpu.roll(more, LANES - offset, 1))
        return value

    for y in range(edge // 2 + 1):
        value = piece(kernel_ref, y)
        value = jnp.where(lane < HALF, value, pltpu.roll(value, HALF, 1))
        value = value + jnp.dot(piece(flipped, (edge - y) % edge), mirror, **exact)
        value = value * (0.5 / float(edge**3))
        for t in range(edge // ROWS):
            at = pl.ds(t * ROWS * height + y, ROWS, stride=height)
            out_ref[at, :] = value[t * ROWS : (t + 1) * ROWS]


def screen_terms(numbers, kernel):
    edge, plane = kernel.shape
    smem = pl.BlockSpec(memory_space=pltpu.SMEM)
    vmem = pl.BlockSpec(memory_space=pltpu.VMEM)
    table = jax.ShapeDtypeStruct((6 * LANES, 2 * LANES), jnp.bfloat16)
    return pl.pallas_call(
        functools.partial(screen_kernel, edge),
        out_shape=[
            jax.ShapeDtypeStruct((edge * padded_half(edge), LANES), jnp.float32),
            jax.ShapeDtypeStruct(numbers.shape, numbers.dtype),
            table,
            table,
        ],
        in_specs=[smem, vmem, vmem],
        out_specs=[vmem, smem, vmem, vmem],
        scratch_shapes=[pltpu.VMEM((edge, plane), jnp.float32)],
        compiler_params=pltpu.CompilerParams(vmem_limit_bytes=8 << 20),
        name="screen_terms",
    )(numbers, kernel, jnp.asarray(wave_table(edge)))


def pair_kernel(shape, second_part, numbers_ref, *refs):
    edge, orb_dev, groups, fragments, slots = shape
    plane = edge * edge
    chunks = plane // LANES
    tiles = edge // ROWS
    half = edge // 2 + 1
    height = padded_half(edge)
    tables, refs = refs[:3], refs[3:]
    phi_refs, refs = refs[:groups], refs[groups:]
    if second_part:
        (twin_ref, relay_ref, one_ref, act_before, back_before), refs = refs[:5], refs[5:]
        act_outs, back_outs, refs = refs[:2], refs[2:5], refs[5:]
        (act, back, state_sem, out_sem), refs = refs[:4], refs[4:]
    else:
        (twin_ref, two_ref, act), back_outs, refs = refs[:3], refs[3:6], refs[6:]
        (back, out_sem), refs = refs[:2], refs[2:]
    (near, far, wide, moved, dense, lower, upper, masks, listed, load_sem) = refs[:10]
    screen_ref, ahead_ref, behind_ref, table_sem = refs[10:]

    fragment, member, live_slots = numbers_ref[0], numbers_ref[1], numbers_ref[2]

    def first_of(slot):
        return numbers_ref[3 + slot]

    def second_of(slot):
        return numbers_ref[3 + slots + slot]

    def reach_of(slot):
        return numbers_ref[3 + 2 * slots + slot]

    def anchor(place, axis):
        return numbers_ref[3 + 3 * slots + 3 * place + axis]

    table_copies = [
        pltpu.make_async_copy(table, hold, table_sem.at[i])
        for i, (table, hold) in enumerate(zip(tables, refs[10:13]))
    ]
    lane = lax.broadcasted_iota(jnp.int32, (1, LANES), 1)
    stretch = next(n for n in (6, 4, 3, 2, 1) if chunks % n == 0)
    middle = pl.ds(edge, edge)

    even = lax.rem(fragment, 2) == 0

    def is_mine(slot):
        return (slot < live_slots) & (lax.div(second_of(slot), orb_dev) == member)

    def list_farthest(slot, found):
        chosen = is_mine(slot) & (reach_of(slot) == 2)

        @pl.when(chosen)
        def _():
            listed[found] = slot

        return found + chosen.astype(jnp.int32)

    farthest = lax.fori_loop(0, slots, list_farthest, jnp.int32(0))
    room = jnp.maximum(2, 2 * lax.div(farthest + 1, 2)) - farthest

    def list_others(slot, counts):
        early, found = counts
        mine = is_mine(slot) & (reach_of(slot) < 2)
        come = (reach_of(slot) == 0) | (even & (lax.rem(second_of(slot), orb_dev) == 0))
        taken = mine & come & (early < room)
        chosen = mine & jnp.logical_not(taken) if second_part else taken

        @pl.when(chosen)
        def _():
            listed[found] = slot

        return early + taken.astype(jnp.int32), found + chosen.astype(jnp.int32)

    begun = jnp.int32(0) if second_part else farthest
    _, found = lax.fori_loop(0, slots, list_others, (jnp.int32(0), begun))
    turns = lax.div(found + 1, 2)

    def slot_of(turn, side):
        at = 2 * turn + side
        live = at < found
        return listed[jnp.where(live, at, 2 * turn)], live

    def far_copy(side, source):
        return pltpu.make_async_copy(source, far.at[side], load_sem.at[1, side])

    def start_loads(turn):
        for side in range(2):
            slot, _ = slot_of(turn, side)
            first, second, reach = first_of(slot), second_of(slot), reach_of(slot)
            relative = lax.div(first, orb_dev) ^ member
            for k in range(groups):
                @pl.when(relative == k)
                def _():
                    pltpu.make_async_copy(
                        phi_refs[k].at[lax.rem(first, orb_dev)],
                        near.at[lax.rem(turn, 2), side],
                        load_sem.at[0, side],
                    ).start()
            own = lax.rem(second, orb_dev)

            @pl.when(reach == 0)
            def _():
                far_copy(side, phi_refs[0].at[own]).start()

            @pl.when((reach == 1) & (own == 0) & even)
            def _():
                far_copy(side, twin_ref.at[0]).start()

            if not second_part:
                @pl.when(reach == 2)
                def _():
                    far_copy(side, two_ref.at[own]).start()

            if second_part:
                @pl.when((reach == 1) & (own == 0) & jnp.logical_not(even))
                def _():
                    far_copy(side, relay_ref.at[0]).start()

                @pl.when((reach == 1) & (own > 0))
                def _():
                    far_copy(side, one_ref.at[jnp.maximum(own - 1, 0)]).start()

    def wait_loads(turn):
        for side in range(2):
            pltpu.make_async_copy(
                phi_refs[0].at[0], near.at[lax.rem(turn, 2), side], load_sem.at[0, side]
            ).wait()
            far_copy(side, phi_refs[0].at[0]).wait()

    @pl.when(found > 0)
    def _():
        start_loads(0)
        for copy in table_copies:
            copy.start()

    if second_part:
        state_copies = [
            pltpu.make_async_copy(before, now, state_sem.at[i])
            for i, (before, now) in enumerate(((act_before, act), (back_before, back)))
        ]
        slab = plane * edge // LANES // groups
        act_copies = []
        for k in range(groups):
            source = (member ^ k) * slab
            place = reversed_bits(k, groups)
            act_copies.append(
                pltpu.make_async_copy(
                    act.at[:, pl.ds(pl.multiple_of(source, ROWS), slab), :],
                    act_outs[2 * place // groups].at[place % (groups // 2)],
                    out_sem.at[3 + k],
                )
            )
    else:
        act[...] = jnp.zeros_like(act)
        back[...] = jnp.zeros_like(back)

    def offset_of(slot):
        partner = lax.rem(fragment + reach_of(slot), fragments)
        return [anchor(partner, i) - anchor(fragment, i) for i in range(3)]

    def steps(count, body, most):
        width = max(n for n in range(1, most + 1) if count % n == 0)

        def step(i, _):
            for j in range(width):
                body(i * width + j)
            return 0

        if width == count:
            step(0, 0)
        else:
            lax.fori_loop(0, count // width, step, 0)

    def columns(k):
        return pl.ds(pl.multiple_of(k * LANES, LANES), LANES)

    def set_masks(place, delta, weight):
        shape = masks.shape[1:]
        spot = lax.broadcasted_iota(jnp.int32, shape, 0) * LANES
        spot = spot + lax.broadcasted_iota(jnp.int32, shape, 1)
        y = ((spot.astype(jnp.float32) + 0.5) * (1.0 / edge)).astype(jnp.int32)
        z = spot - y * edge - delta[2]
        y = y - delta[1]
        inside = (y >= 0) & (y < edge) & (z >= 0) & (z < edge)
        masks[place] = jnp.where(inside, weight, 0.0)

    def shifted(source, place, delta, begin, count, ks):
        shift = lax.rem(delta[1] * edge + delta[2] + 4 * plane, plane)
        start = lax.rem(plane - shift, plane)
        whole, part = lax.div(start, LANES), lax.rem(start, LANES)
        turn = lax.rem(LANES - part, LANES)
        down = edge - jnp.clip(delta[0], -edge, edge) + begin
        x = lax.broadcasted_iota(jnp.int32, (count, LANES), 0) + (begin - delta[0])
        rows_inside = (x >= 0) & (x < edge)
        first = lane < LANES - part

        def piece(k):
            return pltpu.roll(source[lax.rem(k + whole, chunks), pl.ds(down, count), :], turn, 1)

        out = []
        low = piece(ks[0])
        for k in ks:
            high = piece(k + 1)
            value = jnp.where(first, low, high) * masks[place, pl.ds(k, 1), :]
            out.append(jnp.where(rows_inside, value, 0.0))
            low = high
        return out

    def tile(t, i, size):
        return pl.ds(pl.multiple_of(i * size + t * ROWS, ROWS), ROWS)

    def across(t, i, size):
        return pl.ds(t * (ROWS * size) + i, ROWS, stride=size)

    def solve_two(turn, _):
        wait_loads(turn)
        if second_part:
            @pl.when(turn == 0)
            def _():
                for copy in state_copies:
                    copy.start()

        near_now = near.at[lax.rem(turn, 2)]
        picked = [slot_of(turn, side) for side in range(2)]
        offsets = [offset_of(slot) for slot, _ in picked]
        returns = [[-d for d in delta] for delta in offsets]
        for side in range(2):
            set_masks(side, offsets[side], picked[side][1].astype(jnp.float32))
            set_masks(2 + side, returns[side], 1.0)

        def widen(k):
            for side in range(2):
                wide[side, k, middle, :] = far[side, :, pl.ds(pl.multiple_of(k * LANES, LANES), LANES)]

        steps(chunks, widen, chunks)

        def over_y(t):
            densities = []
            begin = pl.multiple_of(t * ROWS, ROWS)
            rows = pl.ds(begin, ROWS)
            for side in range(2):
                values = shifted(wide.at[side], side, offsets[side], begin, ROWS, range(chunks))
                for k in range(chunks):
                    moved[side, k, rows, :] = values[k]
                    values[k] = values[k] * near_now[side, rows, k * LANES : (k + 1) * LANES]
                densities.append(values)
            planes = []
            for y in range(edge):
                first, offset = divmod(y * edge, LANES)
                sides = []
                for side in range(2):
                    shift = (side * HALF - offset) % LANES
                    value = densities[side][first]
                    value = pltpu.roll(value, shift, 1) if shift else value
                    if offset + edge > LANES:
                        more = densities[side][first + 1]
                        more = pltpu.roll(more, shift, 1) if shift else more
                        value = jnp.where(lane < side * HALF + LANES - offset, value, more)
                    sides.append(value)
                planes.append(Number(jnp.where(lane < HALF, sides[0], sides[1])))
            values = real_dft(planes)
            for i in range(half):
                at = tile(t, i, edge)
                lower[0, at, :] = values[i].real
                imag = values[i].imag
                lower[1, at, :] = jnp.zeros((ROWS, LANES), jnp.float32) if imag is None else imag

        steps(tiles, over_y, 3)

        @pl.when(turn == 0)
        def _():
            for copy in table_copies:
                copy.wait()

        @pl.when(turn + 1 < turns)
        def _():
            start_loads(turn + 1)

        def over_x(t):
            at = [across(t, i, edge) for i in range(edge)]
            values = dft([Number(lower[0, a, :], lower[1, a, :]) for a in at], -1)
            real = jnp.concatenate([value.real for value in values], axis=0)
            imag = jnp.concatenate([value.imag for value in values], axis=0)
            at = [tile(t, i, height) for i in range(edge)]
            factor = jnp.concatenate([screen_ref[a, :] for a in at], axis=0)
            real, imag = split_dot(real, imag, ahead_ref)
            real, imag = split_dot(real * factor, imag * factor, behind_ref)
            rows = [slice(i * ROWS, (i + 1) * ROWS) for i in range(edge)]
            values = dft([Number(real[r], imag[r]) for r in rows], 1)
            for i in range(edge):
                upper[0, at[i], :] = values[i].real
                upper[1, at[i], :] = values[i].imag

        steps(height // ROWS, over_x, 4)
        if second_part:
            @pl.when(turn == 0)
            def _():
                for copy in state_copies:
                    copy.wait()

        firsts = [first_of(slot) for slot, _ in picked]

        def back_y(t):
            begin = pl.multiple_of(t * ROWS, ROWS)
            rows = pl.ds(begin, ROWS)
            at = [across(t, i, height) for i in range(half)]
            values = [Number(upper[0, a, :], upper[1, a, :]) for a in at]
            values = values + [values[edge - i].conj() for i in range(half, edge)]
            planes = real_back(values)
            for side in range(2):
                forward = []
                for k in range(chunks):
                    value = None
                    for y in range(k * LANES // edge, edge):
                        begins = y * edge - k * LANES
                        if begins >= LANES:
                            break
                        shift = (begins - side * HALF) % LANES
                        piece = pltpu.roll(planes[y], shift, 1) if shift else planes[y]
                        value = piece if value is None else jnp.where(lane < begins, value, piece)
                    forward.append(value * moved[side, k, rows, :])
                    other = value * near_now[side, rows, k * LANES : (k + 1) * LANES]
                    dense[side, k, pl.ds(edge + begin, ROWS), :] = other
                at = [pl.ds(t * (ROWS * chunks) + k, ROWS, stride=chunks) for k in range(chunks)]
                sums = [act[firsts[side], at[k], :] + forward[k] for k in range(chunks)]
                for k in range(chunks):
                    act[firsts[side], at[k], :] = sums[k]

        steps(tiles, back_y, 3)

        if second_part:
            @pl.when(turn + 1 == turns)
            def _():
                for copy in act_copies:
                    copy.start()

        homes = []
        for side in range(2):
            slot = picked[side][0]
            homes.append(reach_of(slot) * orb_dev + lax.rem(second_of(slot), orb_dev))

        def send_back(g):
            for side in range(2):
                ks = [g * stretch + i for i in range(stretch)]
                values = shifted(dense.at[side], 2 + side, returns[side], 0, edge, ks)
                at = [
                    (i, t, pl.ds(t * (ROWS * chunks) + ks[i], ROWS, stride=chunks))
                    for i in range(stretch)
                    for t in range(tiles)
                ]
                sums = [
                    back[homes[side], a, :] + values[i][t * ROWS : (t + 1) * ROWS] for i, t, a in at
                ]
                for (i, t, a), value in zip(at, sums):
                    back[homes[side], a, :] = value

        steps(chunks // stretch, send_back, 3)
        return 0

    if second_part:
        @pl.when(found == 0)
        def _():
            for copy in state_copies:
                copy.start()
            for copy in state_copies:
                copy.wait()
            for copy in act_copies:
                copy.start()

    lax.fori_loop(0, turns, solve_two, 0)
    if second_part:
        spans = ((orb_dev, 1), (orb_dev + 1, orb_dev - 1), (0, orb_dev))
    else:
        spans = ((2 * orb_dev + 1, orb_dev - 1), (2 * orb_dev, 1), (0, 2 * orb_dev))
    copies = [
        pltpu.make_async_copy(back.at[pl.ds(begin, count)], back_outs[i], out_sem.at[i])
        for i, (begin, count) in enumerate(spans)
    ]
    for copy in copies:
        copy.start()
    if second_part:
        copies += act_copies
    for copy in copies:
        copy.wait()


def reversed_bits(k, count):
    bits = count.bit_length() - 1
    return sum(((k >> i) & 1) << (bits - 1 - i) for i in range(bits))


def pair_terms(numbers, fragments, slots, tables, pieces, far, before=()):
    second_part = bool(before)
    orb_dev, edge, plane = pieces[0].shape
    groups = len(pieces)
    frag_size = groups * orb_dev
    chunks = plane // LANES
    rows = edge * chunks
    height = padded_half(edge)
    shape = (edge, orb_dev, groups, fragments, slots)
    smem = pl.BlockSpec(memory_space=pltpu.SMEM)
    vmem = pl.BlockSpec(memory_space=pltpu.VMEM)
    hbm = pl.BlockSpec(memory_space=pltpu.HBM)
    f32 = jnp.float32

    def fields(*counts):
        return [jax.ShapeDtypeStruct((count, rows, LANES), f32) for count in counts]

    if second_part:
        out_shape = [jax.ShapeDtypeStruct((groups // 2, frag_size, rows // groups, LANES), f32)] * 2
        out_shape += fields(1, orb_dev - 1, orb_dev)
        out_specs = [hbm] * 5
        scratch = [pltpu.VMEM(field.shape, f32) for field in fields(frag_size, REACH * orb_dev)]
        scratch += [pltpu.SemaphoreType.DMA((2,)), pltpu.SemaphoreType.DMA((3 + groups,))]
    else:
        out_shape = fields(frag_size, orb_dev - 1, 1, REACH * orb_dev)
        out_specs = [vmem, hbm, hbm, hbm]
        scratch = [pltpu.VMEM(((REACH + 1) * orb_dev, rows, LANES), f32)]
        scratch += [pltpu.SemaphoreType.DMA((3,))]
    return pl.pallas_call(
        functools.partial(pair_kernel, shape, second_part),
        out_shape=out_shape,
        in_specs=[smem] + [hbm] * (3 + groups + len(far) + len(before)),
        out_specs=out_specs,
        scratch_shapes=scratch
        + [
            pltpu.VMEM((2, 2, edge, plane), f32),
            pltpu.VMEM((2, edge, plane), f32),
            pltpu.VMEM((2, chunks, 3 * edge, LANES), f32),
            pltpu.VMEM((2, chunks, edge, LANES), f32),
            pltpu.VMEM((2, chunks, 3 * edge, LANES), f32),
            pltpu.VMEM((2, height * edge, LANES), f32),
            pltpu.VMEM((2, height * edge, LANES), f32),
            pltpu.VMEM((4, -(-chunks // ROWS) * ROWS, LANES), f32),
            pltpu.SMEM((slots,), jnp.int32),
            pltpu.SemaphoreType.DMA((2, 2)),
            *[pltpu.VMEM(table.shape, table.dtype) for table in tables],
            pltpu.SemaphoreType.DMA((3,)),
        ],
        compiler_params=pltpu.CompilerParams(vmem_limit_bytes=30 << 20),
        name="late_pair_terms" if second_part else "early_pair_terms",
    )(numbers, *tables, *pieces, *far, *before)


def flatten_kernel(shape, places_ref, *refs):
    edge, orb_dev, groups = shape
    pieces, (flat_ref, slab_ref) = refs[:groups], refs[groups:]
    member = places_ref[1]
    chunks = edge * edge // LANES
    slab = slab_ref.shape[1]
    for k in range(groups):
        for o in range(orb_dev):
            def move(j, _):
                value = pieces[k][o, :, pl.ds(pl.multiple_of(j * LANES, LANES), LANES)]
                for t in range(edge // ROWS):
                    at = pl.ds(t * (ROWS * chunks) + j, ROWS, stride=chunks)
                    flat_ref[k * orb_dev + o, at, :] = value[t * ROWS : (t + 1) * ROWS]
                return 0

            lax.fori_loop(0, chunks, move, 0)
    slab_ref[...] = flat_ref[:, pl.ds(pl.multiple_of(member * slab, ROWS), slab), :]


def flatten_terms(places, pieces):
    orb_dev, edge, plane = pieces[0].shape
    groups = len(pieces)
    rows = edge * plane // LANES
    frag_size = groups * orb_dev
    smem = pl.BlockSpec(memory_space=pltpu.SMEM)
    vmem = pl.BlockSpec(memory_space=pltpu.VMEM)
    return pl.pallas_call(
        functools.partial(flatten_kernel, (edge, orb_dev, groups)),
        out_shape=(
            jax.ShapeDtypeStruct((frag_size, rows, LANES), jnp.float32),
            jax.ShapeDtypeStruct((frag_size, rows // groups, LANES), jnp.float32),
        ),
        in_specs=[smem] + [vmem] * groups,
        out_specs=(vmem, vmem),
        compiler_params=pltpu.CompilerParams(vmem_limit_bytes=24 << 20),
        name="flatten_terms",
    )(places, *pieces)


def products(lefts, rights, length, step):
    def add(i, sums):
        at = pl.ds(pl.multiple_of(i * step, ROWS), step)
        right = [ref[index, at, :].reshape(step // ROWS, ROWS, LANES) for ref, index in rights]
        out = []
        for n, (ref, index) in enumerate(lefts):
            left = ref[index, at, :].reshape(step // ROWS, ROWS, LANES)
            for m in range(len(rights)):
                out.append(sums[n * len(rights) + m] + jnp.sum(left * right[m], axis=0))
        return tuple(out)

    zero = jnp.zeros((ROWS, LANES), jnp.float32)
    return lax.fori_loop(0, length // step, add, (zero,) * (len(lefts) * len(rights)))


def placed(result, sums, rows, lanes):
    row = lax.broadcasted_iota(jnp.int32, result.shape, 0)
    lane = lax.broadcasted_iota(jnp.int32, result.shape, 1)
    for n, a in enumerate(rows):
        for m, b in enumerate(lanes):
            value = jnp.sum(sums[n * len(lanes) + m], keepdims=True)
            result = jnp.where((row == a) & (lane == b), result + value, result)
    return result


def step_of(length):
    return next(n for n in (72, 24, 8) if length % n == 0)


def action_kernel(shape, places_ref, phi_ref, kept_ref, *refs):
    orb_dev, groups, parts = shape
    arrived, (act_ref, share_ref) = refs[:parts], refs[parts:]
    member = places_ref[1]
    frag_size = orb_dev * groups
    slab = act_ref.shape[1]
    cut = frag_size // parts
    for i in range(parts):
        span = slice(i * cut, (i + 1) * cut)
        act_ref[span] = kept_ref[0, span] + arrived[i][0]
    rows = [(member ^ (a // orb_dev)) * orb_dev + a % orb_dev for a in range(frag_size)]
    result = jnp.zeros(share_ref.shape, jnp.float32)
    for half in range(0, frag_size, 4):
        bs = range(half, min(half + 4, frag_size))
        lefts, rights = [(phi_ref, a) for a in range(frag_size)], [(act_ref, b) for b in bs]
        result = placed(result, products(lefts, rights, slab, step_of(slab)), rows, bs)
    share_ref[...] = result


def action_terms(places, orb_dev, phi, kept, arrived):
    frag_size, slab = phi.shape[:2]
    smem = pl.BlockSpec(memory_space=pltpu.SMEM)
    vmem = pl.BlockSpec(memory_space=pltpu.VMEM)
    return pl.pallas_call(
        functools.partial(action_kernel, (orb_dev, frag_size // orb_dev, len(arrived))),
        out_shape=(
            jax.ShapeDtypeStruct((frag_size, slab, LANES), jnp.float32),
            jax.ShapeDtypeStruct((frag_size, LANES), jnp.float32),
        ),
        in_specs=[smem] + [vmem] * (2 + len(arrived)),
        out_specs=(vmem, vmem),
        compiler_params=pltpu.CompilerParams(vmem_limit_bytes=16 << 20),
        name="action_terms",
    )(places, phi, kept, *arrived)


def home_kernel(shape, places_ref, flat_ref, own_ref, *refs):
    edge, orb_dev, groups, first, count = shape
    if first == 0:
        (two_ref, twin_ref, relay_ref, share_ref), refs = refs[:4], refs[4:]
    else:
        (two_ref, one_ref), refs = refs[:2], refs[2:]
    outs, total = refs[:groups], refs[groups]
    fragment, member = places_ref[0], places_ref[1]
    frag_size = orb_dev * groups
    rows = flat_ref.shape[1]
    slab = rows // groups
    for i in range(count):
        value = own_ref[first + i] + two_ref[i]
        if first == 0:
            @pl.when(lax.rem(fragment, 2) == 1)
            def _():
                total[i] = value + twin_ref[i]

            @pl.when(lax.rem(fragment, 2) == 0)
            def _():
                total[i] = value + relay_ref[i]
        else:
            total[i] = value + one_ref[i]
    lefts, rights = [(flat_ref, a) for a in range(frag_size)], [(total, i) for i in range(count)]
    places = [(member ^ (a // orb_dev)) * orb_dev + a % orb_dev for a in range(frag_size)]
    result = share_ref[...] if first == 0 else jnp.zeros((frag_size, LANES), jnp.float32)
    sums = products(lefts, rights, rows, step_of(rows))
    result = placed(result, sums, places, [member * orb_dev + first + i for i in range(count)])
    result = result * (1.0 / float(edge**3))
    for k in range(groups):
        begin = pl.multiple_of((member ^ k) * slab, ROWS)
        for i in range(count):
            outs[k][i * slab : (i + 1) * slab, :] = total[i, pl.ds(begin, slab), :]
        outs[k][count * slab :, :] = result


def home_terms(places, edge, groups, flat, own, first, *came):
    frag_size, rows = flat.shape[:2]
    count = came[0].shape[0]
    smem = pl.BlockSpec(memory_space=pltpu.SMEM)
    vmem = pl.BlockSpec(memory_space=pltpu.VMEM)
    f32 = jnp.float32
    parcel = jax.ShapeDtypeStruct((count * rows // groups + frag_size, LANES), f32)
    return pl.pallas_call(
        functools.partial(home_kernel, (edge, frag_size // groups, groups, first, count)),
        out_shape=[parcel] * groups,
        in_specs=[smem] + [vmem] * (2 + len(came)),
        out_specs=[vmem] * groups,
        scratch_shapes=[pltpu.VMEM((count, rows, LANES), f32)],
        compiler_params=pltpu.CompilerParams(vmem_limit_bytes=16 << 20),
        name="home_terms",
    )(places, flat, own, *came)


def exchanged(value, axis, width):
    size = value.shape[axis]
    index = lax.broadcasted_iota(jnp.int32, value.shape, axis)
    below, above = pltpu.roll(value, width, axis), pltpu.roll(value, size - width, axis)
    return jnp.where((index & width) != 0, below, above)


def gradient_kernel(shape, places_ref, act_ref, phi_ref, *refs):
    edge, orb_dev, groups = shape
    heads, tails, refs = refs[:groups], refs[groups : 2 * groups], refs[2 * groups :]
    out_ref, lagrange_ref, hold = refs
    member = places_ref[1]
    frag_size = orb_dev * groups
    chunks = edge * edge // LANES
    slab_rows = edge // groups
    slab = slab_rows * chunks
    sums = [
        head[slab:, :] + tail[(orb_dev - 1) * slab :, :] for head, tail in zip(heads, tails)
    ]
    while len(sums) > 1:
        sums = [sums[i] + sums[i + 1] for i in range(0, len(sums), 2)]
    square = jnp.concatenate([sums[0], jnp.zeros((LANES - frag_size, LANES), jnp.float32)], axis=0)
    lagrange = 0.5 * (square + square.T)[:frag_size, :]
    lagrange_ref[...] = lagrange[:, :frag_size]
    bit = 1
    while bit < groups:
        turned = exchanged(exchanged(lagrange, 0, bit * orb_dev), 1, bit * orb_dev)
        lagrange = jnp.where((member & bit) != 0, turned, lagrange)
        bit *= 2

    for k in range(groups):
        for o in range(orb_dev):
            a = (member ^ k) * orb_dev + o
            came = heads[k][:slab, :] if o == 0 else tails[k][(o - 1) * slab : o * slab, :]
            value = act_ref[a] + came
            for b in range(frag_size):
                factor = lagrange[b : b + 1, k * orb_dev + o : k * orb_dev + o + 1]
                value = value - factor * phi_ref[b]
            hold[pl.ds(pl.multiple_of(a * slab, ROWS), slab), :] = value
    for x in range(slab_rows):
        for j in range(chunks):
            value = hold[pl.ds(x * chunks + j, frag_size, stride=slab), :]
            out_ref[x, :, j * LANES : (j + 1) * LANES] = value


def gradient_terms(places, edge, act, phi, heads, tails):
    groups = len(heads)
    frag_size, slab = act.shape[:2]
    smem = pl.BlockSpec(memory_space=pltpu.SMEM)
    vmem = pl.BlockSpec(memory_space=pltpu.VMEM)
    f32 = jnp.float32
    gradient, lagrange = pl.pallas_call(
        functools.partial(gradient_kernel, (edge, frag_size // groups, groups)),
        out_shape=(
            jax.ShapeDtypeStruct((edge // groups, frag_size, edge * edge), f32),
            jax.ShapeDtypeStruct((frag_size, frag_size), f32),
        ),
        in_specs=[smem] + [vmem] * (2 + 2 * groups),
        out_specs=(vmem, vmem),
        scratch_shapes=[pltpu.VMEM((frag_size * slab, LANES), f32)],
        compiler_params=pltpu.CompilerParams(vmem_limit_bytes=16 << 20),
        name="gradient_terms",
    )(places, act, phi, *heads, *tails)
    return gradient.transpose(1, 0, 2), lagrange


def together(*arrays):
    return lax.optimization_barrier(arrays)


def to_fragment(block, distance, senders=None):
    devices = lax.axis_size("orb")
    senders = range(devices) if senders is None else range(senders, devices, 2)
    return lax.ppermute(block, "orb", [(i, (i + distance) % devices) for i in senders])


def with_twin(block):
    return lax.ppermute(block, "orb", [(i, i ^ 1) for i in range(lax.axis_size("orb"))])


def with_member(block, bit):
    return lax.ppermute(block, "grp", [(i, i ^ bit) for i in range(lax.axis_size("grp"))])


def by_member(parcels):
    groups = len(parcels)
    received = list(parcels)
    bit = groups // 2
    while bit:
        for k in reversed(range(groups)):
            if k & bit:
                received[k] = with_member(received[k], bit)
        bit //= 2
    return received


def shards(orbitals, kernel, anchors, pair_count, pair_first, pair_second, pair_reach):
    groups = lax.axis_size("grp")
    orb_dev, edge, plane = orbitals.shape
    places = jnp.stack([lax.axis_index("orb"), lax.axis_index("grp")]).astype(jnp.int32)

    numbers = [places, pair_count, pair_first, pair_second, pair_reach, anchors.reshape(-1)]
    screen, numbers, *tables = screen_terms(jnp.concatenate(numbers), kernel)
    two = to_fragment(orbitals, -2)
    twin = with_twin(orbitals[:1])
    pieces = {0: orbitals}
    bit = groups // 2
    while bit:
        for k in list(pieces):
            pieces[k ^ bit] = with_member(pieces[k], bit)
        if bit == groups // 2:
            two, twin, tail, pieces[bit], screen, numbers, *tables = together(
                two, twin, orbitals[1:], pieces[bit], screen, numbers, *tables
            )
            one = to_fragment(tail, -1)
            relay = to_fragment(twin, -2, 1)
        bit //= 2
    pieces = [pieces[k] for k in range(groups)]
    tables = [screen, *tables]
    sizes = (anchors.shape[0], pair_first.shape[0])
    act, two_tail, two_head, back = pair_terms(numbers, *sizes, tables, pieces, [twin, two])
    two_tail = to_fragment(two_tail, 2)
    kept, sent, one_head, one_tail, own = pair_terms(
        numbers, *sizes, tables, pieces, [twin, relay, one], [act, back]
    )

    sent, two_tail, two_head = together(sent, two_tail, two_head)
    two_head = to_fragment(two_head, 2)
    twin = with_twin(one_head)
    bit = 1
    arrived = with_member(sent, bit)
    while 2 * bit < groups:
        kept = kept + arrived
        if bit == 1:
            _, twin, one_tail, two_head = together(kept, twin, one_tail, two_head)
        half = kept.shape[0] // 2
        bit *= 2
        arrived, kept = with_member(kept[half:], bit), kept[:half]
    one_tail = to_fragment(one_tail, 1)
    relay = to_fragment(twin, 2, 0)

    flat, phi = flatten_terms(places, pieces)
    tails = home_terms(places, edge, groups, flat, own, 1, two_tail, one_tail)
    tails = by_member(tails)
    act, share = action_terms(places, orb_dev, phi, kept, [arrived])
    heads = by_member(
        home_terms(places, edge, groups, flat, own, 0, two_head, twin, relay, share)
    )
    gradient, lagrange = gradient_terms(places, edge, act, phi, heads, tails)
    return (gradient, lagrange[None])


def solution(mesh):
    placed = (P(("orb", "grp"), None, None), P(), P(), P("orb"), P("orb"), P("orb"), P("orb"))
    return jax.shard_map(
        shards,
        mesh=mesh,
        in_specs=placed,
        out_specs=(P("orb", "grp", None), P("orb", None, None)),
        check_vma=False,
    )
```

profile of v0, /device:TPU:0, one launch (start us, length us, event | category | flops | bytes accessed | tf_op | source)
XLA Modules:
  0.0 106.4 jit_solution(1317054542061816943)
XLA Ops:
  0.7 5.1 %collective-permute-start.1 = (f32[2,48,2304]{2,1,0:T(8,128)}, f32[2,48,2304]{2,1,0:T(8,128)}, u32[]{:S(2)}, u32[]{:S(2)}) collective-permute-start(f32[2,48,2304]{2,1,0:T(8,128)} %refs_3_.3), channel_id=1, source_target_pairs={{0,24},{4,28},{8,0},{12,4},{16,8},{20,12},{24,16},{28,20},{1,25},{... | collective-permute-start | bytes 2654216 | tf_op jit(solution)/shard_map/ppermute | solution.py:993
  5.8 1.5 %collective-permute-start.3 = (f32[2,48,2304]{2,1,0:T(8,128)}, f32[2,48,2304]{2,1,0:T(8,128)S(1)}, u32[]{:S(2)}, u32[]{:S(2)}) collective-permute-start(f32[2,48,2304]{2,1,0:T(8,128)} %refs_3_.3), channel_id=1, source_target_pairs={{0,2},{1,3},{2,0},{3,1},{4,6},{5,7},{6,4},{7,5},{8,10},{9,11},{10,... | collective-permute-start | bytes 2654216 | tf_op jit(solution)/shard_map/ppermute | solution.py:1001
  7.3 2.1 %fusion.1 = (f32[1,48,2304]{2,1,0:T(8,128)}, f32[1,48,2304]{2,1,0:T(8,128)}) fusion(f32[2,48,2304]{2,1,0:T(8,128)} %refs_3_.3), kind=kLoop, calls=%fused_computation.2 | loop fusion | bytes 1769472 | tf_op jit(solution)/shard_map/slice | solution.py:1032
  9.4 1.5 %collective-permute-start.2 = (f32[1,48,2304]{2,1,0:T(8,128)}, f32[1,48,2304]{2,1,0:T(8,128)S(1)}, u32[]{:S(2)}, u32[]{:S(2)}) collective-permute-start(f32[1,48,2304]{2,1,0:T(8,128)} %get-tuple-element.87), channel_id=1, source_target_pairs={{0,4},{4,0},{8,12},{12,8},{16,20},{20,16},{24,28},{28,24},{1,5},{5... | collective-permute-start | bytes 1327112 | tf_op jit(solution)/shard_map/ppermute | solution.py:997
  11.8 0.7 concatenate.4.numbers_ref
  12.5 0.9 copy-done.2
  13.4 3.5 %screen_terms.1 = (f32[1536,128]{1,0:T(8,128)S(1)}, s32[51]{0:T(128)S(1)}, bf16[768,256]{1,0:T(8,128)(2,1)S(1)}, bf16[768,256]{1,0:T(8,128)(2,1)S(1)}) custom-call(s32[51]{0:T(128)S(1)} %concatenate.4.numbers_ref, f32[48,2304]{1,0:T(8,128)S(1)} %copy-done.1, bf16[2,2,128,128]{3,2,1,0:T(8,128)(2,1)S(1)} %copy-done.2), custom_call_target="tpu_custom_call" | custom-call | tf_op jit(solution)/shard_map/screen_terms/pallas_call | solution.py:304
  17.0 4.0 %collective-permute-done.2.refs_7_ = f32[1,48,2304]{2,1,0:T(8,128)S(1)} collective-permute-done((f32[1,48,2304]{2,1,0:T(8,128)}, f32[1,48,2304]{2,1,0:T(8,128)S(1)}, u32[]{:S(2)}, u32[]{:S(2)}) %collective-permute-start.2) | collective-permute-done | bytes 442400 | tf_op jit(solution)/shard_map/ppermute | solution.py:997
  21.0 4.0 %collective-permute-done.1.refs_8_ = f32[2,48,2304]{2,1,0:T(8,128)} collective-permute-done((f32[2,48,2304]{2,1,0:T(8,128)}, f32[2,48,2304]{2,1,0:T(8,128)}, u32[]{:S(2)}, u32[]{:S(2)}) %collective-permute-start.1) | collective-permute-done | bytes 884768 | tf_op jit(solution)/shard_map/ppermute | solution.py:993
  25.0 2.1 %collective-permute-done.3.refs_2_.refs_5_ = f32[2,48,2304]{2,1,0:T(8,128)S(1)} collective-permute-done((f32[2,48,2304]{2,1,0:T(8,128)}, f32[2,48,2304]{2,1,0:T(8,128)S(1)}, u32[]{:S(2)}, u32[]{:S(2)}) %collective-permute-start.3) | collective-permute-done | bytes 884768 | tf_op jit(solution)/shard_map/ppermute | solution.py:1001
  27.1 0.7 collective-permute-start.5
  27.8 4.4 %collective-permute-start.6 = (f32[1,48,2304]{2,1,0:T(8,128)}, f32[1,48,2304]{2,1,0:T(8,128)S(1)}, u32[]{:S(2)}, u32[]{:S(2)}) collective-permute-start(f32[1,48,2304]{2,1,0:T(8,128)} %get-tuple-element.54), channel_id=1, source_target_pairs={{0,28},{4,0},{8,4},{12,8},{16,12},{20,16},{24,20},{28,24},{1,29},{... | collective-permute-start | bytes 1327112 | tf_op jit(solution)/shard_map/ppermute | solution.py:993
  32.2 9.8 %early_pair_terms.1 = (f32[8,864,128]{2,1,0:T(8,128)S(1)}, f32[1,864,128]{2,1,0:T(8,128)S(1)}, f32[1,864,128]{2,1,0:T(8,128)S(1)}, f32[4,864,128]{2,1,0:T(8,128)S(1)}) custom-call(s32[51]{0:T(128)S(1)} %get-tuple-element.49.numbers_ref, f32[1536,128]{1,0:T(8,128)S(1)} %get-tuple-element.50.refs_0_, bf16[768,256]{1,0:T(8,128)(2,1)S(1)} %get-tuple-element.51.refs_1_, ...), custom_call_target="tpu_custom_call" | custom-call | tf_op jit(solution)/shard_map/early_pair_terms/pallas_call | solution.py:737
  42.0 2.4 %collective-permute-start.7 = (f32[1,864,128]{2,1,0:T(8,128)S(1)}, f32[1,864,128]{2,1,0:T(8,128)S(1)}, u32[]{:S(2)}, u32[]{:S(2)}) collective-permute-start(f32[1,864,128]{2,1,0:T(8,128)S(1)} %get-tuple-element.60), channel_id=1, source_target_pairs={{0,8},{4,12},{8,16},{12,20},{16,24},{20,28},{24,0},{28,4},{1,9},{5... | collective-permute-start | bytes 1327112 | tf_op jit(solution)/shard_map/ppermute | solution.py:993
  44.4 3.1 %late_pair_terms.1 = (f32[2,8,216,128]{3,2,1,0:T(8,128)S(1)}, f32[2,8,216,128]{3,2,1,0:T(8,128)S(1)}, f32[1,864,128]{2,1,0:T(8,128)S(1)}, f32[1,864,128]{2,1,0:T(8,128)S(1)}, f32[2,864,128]{2,1,0:T(8,128)S(1)}) custom-call(s32[51]{0:T(128)S(1)} %get-tuple-element.49.numbers_ref, f32[1536,128]{1,0:T(8,128)S(1)} %get-tuple-element.50.refs_0_, ...), custom_call_target="tpu_custom_call" | custom-call | tf_op jit(solution)/shard_map/late_pair_terms/pallas_call | solution.py:737
  47.5 6.1 %collective-permute-done.7.refs_0_ = f32[1,864,128]{2,1,0:T(8,128)S(1)} collective-permute-done((f32[1,864,128]{2,1,0:T(8,128)S(1)}, f32[1,864,128]{2,1,0:T(8,128)S(1)}, u32[]{:S(2)}, u32[]{:S(2)}) %collective-permute-start.7) | collective-permute-done | bytes 442400 | tf_op jit(solution)/shard_map/ppermute | solution.py:993
  53.6 5.3 %collective-permute-start.10 = (f32[1,864,128]{2,1,0:T(8,128)S(1)}, f32[1,864,128]{2,1,0:T(8,128)S(1)}, u32[]{:S(2)}, u32[]{:S(2)}) collective-permute-start(f32[1,864,128]{2,1,0:T(8,128)S(1)} %get-tuple-element.66), channel_id=1, source_target_pairs={{0,4},{4,0},{8,12},{12,8},{16,20},{20,16},{24,28},{28,24},{1,5},{5... | collective-permute-start | bytes 1327112 | tf_op jit(solution)/shard_map/ppermute | solution.py:997
  58.9 7.0 %collective-permute-start.11 = (f32[1,864,128]{2,1,0:T(8,128)S(1)}, f32[1,864,128]{2,1,0:T(8,128)S(1)}, u32[]{:S(2)}, u32[]{:S(2)}) collective-permute-start(f32[1,864,128]{2,1,0:T(8,128)S(1)} %get-tuple-element.68), channel_id=1, source_target_pairs={{0,8},{4,12},{8,16},{12,20},{16,24},{20,28},{24,0},{28,4},{1,9},{5... | collective-permute-start | bytes 1327112 | tf_op jit(solution)/shard_map/ppermute | solution.py:993
  66.3 3.4 %collective-permute-done.10.refs_1_ = f32[1,864,128]{2,1,0:T(8,128)S(1)} collective-permute-done((f32[1,864,128]{2,1,0:T(8,128)S(1)}, f32[1,864,128]{2,1,0:T(8,128)S(1)}, u32[]{:S(2)}, u32[]{:S(2)}) %collective-permute-start.10) | collective-permute-done | bytes 442400 | tf_op jit(solution)/shard_map/ppermute | solution.py:997
  69.7 5.6 %collective-permute-done.11.refs_0_ = f32[1,864,128]{2,1,0:T(8,128)S(1)} collective-permute-done((f32[1,864,128]{2,1,0:T(8,128)S(1)}, f32[1,864,128]{2,1,0:T(8,128)S(1)}, u32[]{:S(2)}, u32[]{:S(2)}) %collective-permute-start.11) | collective-permute-done | bytes 442400 | tf_op jit(solution)/shard_map/ppermute | solution.py:993
  75.6 4.4 %collective-permute-start.12 = (f32[1,864,128]{2,1,0:T(8,128)S(1)}, f32[1,864,128]{2,1,0:T(8,128)S(1)}, u32[]{:S(2)}, u32[]{:S(2)}) collective-permute-start(f32[1,864,128]{2,1,0:T(8,128)S(1)} %collective-permute-done.10.refs_1_), channel_id=1, source_target_pairs={{0,8},{8,16},{16,24},{24,0},{1,9},{9,17},{17,25},{25,1},{2,10},{10... | collective-permute-start | bytes 1327112 | tf_op jit(solution)/shard_map/ppermute | solution.py:993
  80.1 1.5 %flatten_terms.1 = (f32[8,864,128]{2,1,0:T(8,128)S(1)}, f32[8,216,128]{2,1,0:T(8,128)S(1)}) custom-call(s32[2]{0:T(128)S(1)} %pad_add_fusion.places_ref, f32[2,48,2304]{2,1,0:T(8,128)S(1)} %copy-done, f32[2,48,2304]{2,1,0:T(8,128)S(1)} %collective-permute-done.refs_1_.refs_4_, f32[2,48,2304]{2,1,0:T(8,128)S(1)} %collective-permute-done.3.refs_2_.refs_5_, ...), custom_call_target="tpu_custom_call" | custom-call | tf_op jit(solution)/shard_map/flatten_terms/pallas_call | solution.py:788
  81.6 7.4 %collective-permute-done.17.refs_1_ = f32[1,864,128]{2,1,0:T(8,128)S(1)} collective-permute-done((f32[1,864,128]{2,1,0:T(8,128)S(1)}, f32[1,864,128]{2,1,0:T(8,128)S(1)}, u32[]{:S(2)}, u32[]{:S(2)}) %collective-permute-start.17) | collective-permute-done | bytes 442400 | tf_op jit(solution)/shard_map/ppermute | solution.py:993
  89.0 1.1 %home_terms.3 = (f32[224,128]{1,0:T(8,128)S(1)}, f32[224,128]{1,0:T(8,128)S(1)}, f32[224,128]{1,0:T(8,128)S(1)}, f32[224,128]{1,0:T(8,128)S(1)}) custom-call(s32[2]{0:T(128)S(1)} %pad_add_fusion.places_ref, f32[8,864,128]{2,1,0:T(8,128)S(1)} %get-tuple-element.64.flat_ref, f32[2,864,128]{2,1,0:T(8,128)S(1)} %get-tuple-element.65.own_ref, ...), custom_call_target="tpu_custom_call" | custom-call | tf_op jit(solution)/shard_map/home_terms/pallas_call | solution.py:909
  90.2 1.6 %action_terms.1 = (f32[8,216,128]{2,1,0:T(8,128)S(1)}, f32[8,128]{1,0:T(8,128)S(1)}) custom-call(s32[2]{0:T(128)S(1)} %pad_add_fusion.places_ref, f32[8,216,128]{2,1,0:T(8,128)S(1)} %get-tuple-element.48.phi_ref, f32[1,8,216,128]{3,2,1,0:T(8,128)S(1)} %get-tuple-element.85.kept_ref, f32[1,8,216,128]{3,2,1,0:T(8,128)S(1)} %collective-permute-done.9.refs_0_), custom_call_target="tpu_custom_call" | custom-call | tf_op jit(solution)/shard_map/action_terms/pallas_call | solution.py:853
  91.8 1.1 %home_terms.2 = (f32[224,128]{1,0:T(8,128)S(1)}, f32[224,128]{1,0:T(8,128)S(1)}, f32[224,128]{1,0:T(8,128)S(1)}, f32[224,128]{1,0:T(8,128)S(1)}) custom-call(s32[2]{0:T(128)S(1)} %pad_add_fusion.places_ref, f32[8,864,128]{2,1,0:T(8,128)S(1)} %get-tuple-element.64.flat_ref, f32[2,864,128]{2,1,0:T(8,128)S(1)} %get-tuple-element.65.own_ref, ...), custom_call_target="tpu_custom_call" | custom-call | tf_op jit(solution)/shard_map/home_terms/pallas_call | solution.py:909
  93.0 2.0 %collective-permute-start.15 = (f32[224,128]{1,0:T(8,128)S(1)}, f32[224,128]{1,0:T(8,128)S(1)}, u32[]{:S(2)}, u32[]{:S(2)}) collective-permute-start(f32[224,128]{1,0:T(8,128)S(1)} %get-tuple-element.75), channel_id=1, source_target_pairs={{0,2},{1,3},{2,0},{3,1},{4,6},{5,7},{6,4},{7,5},{8,10},{9,11},{10,... | collective-permute-start | bytes 344072 | tf_op jit(solution)/shard_map/ppermute | solution.py:1001
  95.6 1.9 %collective-permute-start.14 = (f32[224,128]{1,0:T(8,128)S(1)}, f32[224,128]{1,0:T(8,128)S(1)}, u32[]{:S(2)}, u32[]{:S(2)}) collective-permute-start(f32[224,128]{1,0:T(8,128)S(1)} %get-tuple-element.74), channel_id=1, source_target_pairs={{0,2},{1,3},{2,0},{3,1},{4,6},{5,7},{6,4},{7,5},{8,10},{9,11},{10,... | collective-permute-start | bytes 344072 | tf_op jit(solution)/shard_map/ppermute | solution.py:1001
  97.5 1.5 %collective-permute-done.15 = f32[224,128]{1,0:T(8,128)S(1)} collective-permute-done((f32[224,128]{1,0:T(8,128)S(1)}, f32[224,128]{1,0:T(8,128)S(1)}, u32[]{:S(2)}, u32[]{:S(2)}) %collective-permute-start.15) | collective-permute-done | bytes 114720 | tf_op jit(solution)/shard_map/ppermute | solution.py:1001
  99.0 2.5 %collective-permute-done.19.refs_6_ = f32[224,128]{1,0:T(8,128)S(1)} collective-permute-done((f32[224,128]{1,0:T(8,128)S(1)}, f32[224,128]{1,0:T(8,128)S(1)}, u32[]{:S(2)}, u32[]{:S(2)}) %collective-permute-start.19) | collective-permute-done | bytes 114720 | tf_op jit(solution)/shard_map/ppermute | solution.py:1001
  101.5 2.2 %collective-permute-done.14.refs_2_ = f32[224,128]{1,0:T(8,128)S(1)} collective-permute-done((f32[224,128]{1,0:T(8,128)S(1)}, f32[224,128]{1,0:T(8,128)S(1)}, u32[]{:S(2)}, u32[]{:S(2)}) %collective-permute-start.14) | collective-permute-done | bytes 114720 | tf_op jit(solution)/shard_map/ppermute | solution.py:1001
  103.7 2.7 %gradient_terms.1 = (f32[12,8,2304]{2,1,0:T(8,128)}, f32[8,8]{1,0:T(8,128)}) custom-call(s32[2]{0:T(128)S(1)} %pad_add_fusion.places_ref, f32[8,216,128]{2,1,0:T(8,128)S(1)} %get-tuple-element.63.act_ref, f32[8,216,128]{2,1,0:T(8,128)S(1)} %get-tuple-element.48.phi_ref, f32[224,128]{1,0:T(8,128)S(1)} %get-tuple-element.72.refs_0_, ...), custom_call_target="tpu_custom_call" | custom-call | tf_op jit(solution)/shard_map/gradient_terms/pallas_call | solution.py:971
  (39 shorter events, 1.8 us)
Async XLA Ops:
  0.6 10.3 %copy-start = (f32[2,48,2304]{2,1,0:T(8,128)S(1)}, f32[2,48,2304]{2,1,0:T(8,128)}, u32[]{:S(2)}) copy-start(f32[2,48,2304]{2,1,0:T(8,128)} %refs_3_.3) | copy-start | bytes 2654212
  0.6 10.3 %copy-start.3 = (s32[8,3]{0,1:T(4,128)S(1)}, s32[8,3]{0,1:T(4,128)}, u32[]{:S(2)}) copy-start(s32[8,3]{0,1:T(4,128)} %param.10) | copy-start | bytes 292
  0.7 11.1 %copy-start.4 = (s32[8]{0:T(128)S(1)}, s32[8]{0:T(128)}, u32[]{:S(2)}) copy-start(s32[8]{0:T(128)} %param.12) | copy-start | bytes 100
  0.7 11.1 %copy-start.5 = (s32[8]{0:T(128)S(1)}, s32[8]{0:T(128)}, u32[]{:S(2)}) copy-start(s32[8]{0:T(128)} %param.13) | copy-start | bytes 100
  0.7 11.8 %copy-start.1 = (f32[48,2304]{1,0:T(8,128)S(1)}, f32[48,2304]{1,0:T(8,128)}, u32[]{:S(2)}) copy-start(f32[48,2304]{1,0:T(8,128)} %kernel_ref.1) | copy-start | bytes 1327108
  0.7 24.3 %collective-permute-start.1 = (f32[2,48,2304]{2,1,0:T(8,128)}, f32[2,48,2304]{2,1,0:T(8,128)}, u32[]{:S(2)}, u32[]{:S(2)}) collective-permute-start(f32[2,48,2304]{2,1,0:T(8,128)} %refs_3_.3), channel_id=1, source_target_pairs={{0,24},{4,28},{8,0},{12,4},{16,8},{20,12},{24,16},{28,20},{1,25},{... | collective-permute-start | bytes 2654216 | tf_op jit(solution)/shard_map/ppermute | solution.py:993
  5.8 21.3 %collective-permute-start.3 = (f32[2,48,2304]{2,1,0:T(8,128)}, f32[2,48,2304]{2,1,0:T(8,128)S(1)}, u32[]{:S(2)}, u32[]{:S(2)}) collective-permute-start(f32[2,48,2304]{2,1,0:T(8,128)} %refs_3_.3), channel_id=1, source_target_pairs={{0,2},{1,3},{2,0},{3,1},{4,6},{5,7},{6,4},{7,5},{8,10},{9,11},{10,... | collective-permute-start | bytes 2654216 | tf_op jit(solution)/shard_map/ppermute | solution.py:1001
  9.4 11.6 %collective-permute-start.2 = (f32[1,48,2304]{2,1,0:T(8,128)}, f32[1,48,2304]{2,1,0:T(8,128)S(1)}, u32[]{:S(2)}, u32[]{:S(2)}) collective-permute-start(f32[1,48,2304]{2,1,0:T(8,128)} %get-tuple-element.87), channel_id=1, source_target_pairs={{0,4},{4,0},{8,12},{12,8},{16,20},{20,16},{24,28},{28,24},{1,5},{5... | collective-permute-start | bytes 1327112 | tf_op jit(solution)/shard_map/ppermute | solution.py:997
  10.9 21.3 %collective-permute-start = (f32[2,48,2304]{2,1,0:T(8,128)S(1)}, f32[2,48,2304]{2,1,0:T(8,128)S(1)}, u32[]{:S(2)}, u32[]{:S(2)}) collective-permute-start(f32[2,48,2304]{2,1,0:T(8,128)S(1)} %copy-done), channel_id=1, source_target_pairs={{0,1},{1,0},{2,3},{3,2},{4,5},{5,4},{6,7},{7,6},{8,9},{9,8},{10,11... | collective-permute-start | bytes 2654216 | tf_op jit(solution)/shard_map/ppermute | solution.py:1001
  12.5 0.9 copy-start.2
  27.1 5.1 %collective-permute-start.4 = (f32[2,48,2304]{2,1,0:T(8,128)S(1)}, f32[2,48,2304]{2,1,0:T(8,128)S(1)}, u32[]{:S(2)}, u32[]{:S(2)}) collective-permute-start(f32[2,48,2304]{2,1,0:T(8,128)S(1)} %collective-permute-done.3.refs_2_.refs_5_), channel_id=1, source_target_pairs={{0,1},{1,0},{2,3},{3,2},{4,5},{5,4},{6,7},{7,6},{8,9},{9,8},{10,11... | collective-permute-start | bytes 2654216 | tf_op jit(solution)/shard_map/ppermute | solution.py:1001
  27.1 17.3 %collective-permute-start.5 = (f32[1,48,2304]{2,1,0:T(8,128)S(1)}, f32[1,48,2304]{2,1,0:T(8,128)S(1)}, u32[]{:S(2)}, u32[]{:S(2)}) collective-permute-start(f32[1,48,2304]{2,1,0:T(8,128)S(1)} %collective-permute-done.2.refs_7_), channel_id=1, source_target_pairs={{4,28},{12,4},{20,12},{28,20},{5,29},{13,5},{21,13},{29,21},{6,30}... | collective-permute-start | bytes 1327112 | tf_op jit(solution)/shard_map/ppermute | solution.py:993
  27.8 16.6 %collective-permute-start.6 = (f32[1,48,2304]{2,1,0:T(8,128)}, f32[1,48,2304]{2,1,0:T(8,128)S(1)}, u32[]{:S(2)}, u32[]{:S(2)}) collective-permute-start(f32[1,48,2304]{2,1,0:T(8,128)} %get-tuple-element.54), channel_id=1, source_target_pairs={{0,28},{4,0},{8,4},{12,8},{16,12},{20,16},{24,20},{28,24},{1,29},{... | collective-permute-start | bytes 1327112 | tf_op jit(solution)/shard_map/ppermute | solution.py:993
  42.0 11.6 %collective-permute-start.7 = (f32[1,864,128]{2,1,0:T(8,128)S(1)}, f32[1,864,128]{2,1,0:T(8,128)S(1)}, u32[]{:S(2)}, u32[]{:S(2)}) collective-permute-start(f32[1,864,128]{2,1,0:T(8,128)S(1)} %get-tuple-element.60), channel_id=1, source_target_pairs={{0,8},{4,12},{8,16},{12,20},{16,24},{20,28},{24,0},{28,4},{1,9},{5... | collective-permute-start | bytes 1327112 | tf_op jit(solution)/shard_map/ppermute | solution.py:993
  53.6 12.3 %collective-permute-start.8 = (f32[2,8,216,128]{3,2,1,0:T(8,128)S(1)}, f32[2,8,216,128]{3,2,1,0:T(8,128)S(1)}, u32[]{:S(2)}, u32[]{:S(2)}) collective-permute-start(f32[2,8,216,128]{3,2,1,0:T(8,128)S(1)} %get-tuple-element.62), channel_id=1, source_target_pairs={{0,1},{1,0},{2,3},{3,2},{4,5},{5,4},{6,7},{7,6},{8,9},{9,8},{10,11... | collective-permute-start | bytes 5308424 | tf_op jit(solution)/shard_map/ppermute | solution.py:1001
  53.6 16.0 %collective-permute-start.10 = (f32[1,864,128]{2,1,0:T(8,128)S(1)}, f32[1,864,128]{2,1,0:T(8,128)S(1)}, u32[]{:S(2)}, u32[]{:S(2)}) collective-permute-start(f32[1,864,128]{2,1,0:T(8,128)S(1)} %get-tuple-element.66), channel_id=1, source_target_pairs={{0,4},{4,0},{8,12},{12,8},{16,20},{20,16},{24,28},{28,24},{1,5},{5... | collective-permute-start | bytes 1327112 | tf_op jit(solution)/shard_map/ppermute | solution.py:997
  58.9 16.4 %collective-permute-start.11 = (f32[1,864,128]{2,1,0:T(8,128)S(1)}, f32[1,864,128]{2,1,0:T(8,128)S(1)}, u32[]{:S(2)}, u32[]{:S(2)}) collective-permute-start(f32[1,864,128]{2,1,0:T(8,128)S(1)} %get-tuple-element.68), channel_id=1, source_target_pairs={{0,8},{4,12},{8,16},{12,20},{16,24},{20,28},{24,0},{28,4},{1,9},{5... | collective-permute-start | bytes 1327112 | tf_op jit(solution)/shard_map/ppermute | solution.py:993
  66.2 24.0 %collective-permute-start.9 = (f32[1,8,216,128]{3,2,1,0:T(8,128)S(1)}, f32[1,8,216,128]{3,2,1,0:T(8,128)S(1)}, u32[]{:S(2)}, u32[]{:S(2)}) collective-permute-start(f32[1,8,216,128]{3,2,1,0:T(8,128)S(1)} %get-tuple-element.84), channel_id=1, source_target_pairs={{0,2},{1,3},{2,0},{3,1},{4,6},{5,7},{6,4},{7,5},{8,10},{9,11},{10,... | collective-permute-start | bytes 2654216 | tf_op jit(solution)/shard_map/ppermute | solution.py:1001
  75.3 13.7 %collective-permute-start.17 = (f32[1,864,128]{2,1,0:T(8,128)S(1)}, f32[1,864,128]{2,1,0:T(8,128)S(1)}, u32[]{:S(2)}, u32[]{:S(2)}) collective-permute-start(f32[1,864,128]{2,1,0:T(8,128)S(1)} %get-tuple-element.77), channel_id=1, source_target_pairs={{0,4},{4,8},{8,12},{12,16},{16,20},{20,24},{24,28},{28,0},{1,5},{5... | collective-permute-start | bytes 1327112 | tf_op jit(solution)/shard_map/ppermute | solution.py:993
  75.6 16.2 %collective-permute-start.12 = (f32[1,864,128]{2,1,0:T(8,128)S(1)}, f32[1,864,128]{2,1,0:T(8,128)S(1)}, u32[]{:S(2)}, u32[]{:S(2)}) collective-permute-start(f32[1,864,128]{2,1,0:T(8,128)S(1)} %collective-permute-done.10.refs_1_), channel_id=1, source_target_pairs={{0,8},{8,16},{16,24},{24,0},{1,9},{9,17},{17,25},{25,1},{2,10},{10... | collective-permute-start | bytes 1327112 | tf_op jit(solution)/shard_map/ppermute | solution.py:993
  90.1 5.0 %collective-permute-start.20 = (f32[224,128]{1,0:T(8,128)S(1)}, f32[224,128]{1,0:T(8,128)S(1)}, u32[]{:S(2)}, u32[]{:S(2)}) collective-permute-start(f32[224,128]{1,0:T(8,128)S(1)} %get-tuple-element.81), channel_id=1, source_target_pairs={{0,2},{1,3},{2,0},{3,1},{4,6},{5,7},{6,4},{7,5},{8,10},{9,11},{10,... | collective-permute-start | bytes 344072 | tf_op jit(solution)/shard_map/ppermute | solution.py:1001
  90.1 5.4 %collective-permute-start.18 = (f32[224,128]{1,0:T(8,128)S(1)}, f32[224,128]{1,0:T(8,128)S(1)}, u32[]{:S(2)}, u32[]{:S(2)}) collective-permute-start(f32[224,128]{1,0:T(8,128)S(1)} %get-tuple-element.79), channel_id=1, source_target_pairs={{0,1},{1,0},{2,3},{3,2},{4,5},{5,4},{6,7},{7,6},{8,9},{9,8},{10,11... | collective-permute-start | bytes 344072 | tf_op jit(solution)/shard_map/ppermute | solution.py:1001
  93.0 6.1 %collective-permute-start.15 = (f32[224,128]{1,0:T(8,128)S(1)}, f32[224,128]{1,0:T(8,128)S(1)}, u32[]{:S(2)}, u32[]{:S(2)}) collective-permute-start(f32[224,128]{1,0:T(8,128)S(1)} %get-tuple-element.75), channel_id=1, source_target_pairs={{0,2},{1,3},{2,0},{3,1},{4,6},{5,7},{6,4},{7,5},{8,10},{9,11},{10,... | collective-permute-start | bytes 344072 | tf_op jit(solution)/shard_map/ppermute | solution.py:1001
  95.0 6.5 %collective-permute-start.19 = (f32[224,128]{1,0:T(8,128)S(1)}, f32[224,128]{1,0:T(8,128)S(1)}, u32[]{:S(2)}, u32[]{:S(2)}) collective-permute-start(f32[224,128]{1,0:T(8,128)S(1)} %get-tuple-element.80), channel_id=1, source_target_pairs={{0,2},{1,3},{2,0},{3,1},{4,6},{5,7},{6,4},{7,5},{8,10},{9,11},{10,... | collective-permute-start | bytes 344072 | tf_op jit(solution)/shard_map/ppermute | solution.py:1001
  95.1 6.4 %collective-permute-start.21 = (f32[224,128]{1,0:T(8,128)S(1)}, f32[224,128]{1,0:T(8,128)S(1)}, u32[]{:S(2)}, u32[]{:S(2)}) collective-permute-start(f32[224,128]{1,0:T(8,128)S(1)} %collective-permute-done.20), channel_id=1, source_target_pairs={{0,1},{1,0},{2,3},{3,2},{4,5},{5,4},{6,7},{7,6},{8,9},{9,8},{10,11... | collective-permute-start | bytes 344072 | tf_op jit(solution)/shard_map/ppermute | solution.py:1001
  95.3 6.2 %collective-permute-start.13 = (f32[224,128]{1,0:T(8,128)S(1)}, f32[224,128]{1,0:T(8,128)S(1)}, u32[]{:S(2)}, u32[]{:S(2)}) collective-permute-start(f32[224,128]{1,0:T(8,128)S(1)} %get-tuple-element.73), channel_id=1, source_target_pairs={{0,1},{1,0},{2,3},{3,2},{4,5},{5,4},{6,7},{7,6},{8,9},{9,8},{10,11... | collective-permute-start | bytes 344072 | tf_op jit(solution)/shard_map/ppermute | solution.py:1001
  95.6 8.1 %collective-permute-start.14 = (f32[224,128]{1,0:T(8,128)S(1)}, f32[224,128]{1,0:T(8,128)S(1)}, u32[]{:S(2)}, u32[]{:S(2)}) collective-permute-start(f32[224,128]{1,0:T(8,128)S(1)} %get-tuple-element.74), channel_id=1, source_target_pairs={{0,2},{1,3},{2,0},{3,1},{4,6},{5,7},{6,4},{7,5},{8,10},{9,11},{10,... | collective-permute-start | bytes 344072 | tf_op jit(solution)/shard_map/ppermute | solution.py:1001
  99.0 4.6 %collective-permute-start.16 = (f32[224,128]{1,0:T(8,128)S(1)}, f32[224,128]{1,0:T(8,128)S(1)}, u32[]{:S(2)}, u32[]{:S(2)}) collective-permute-start(f32[224,128]{1,0:T(8,128)S(1)} %collective-permute-done.15), channel_id=1, source_target_pairs={{0,1},{1,0},{2,3},{3,2},{4,5},{5,4},{6,7},{7,6},{8,9},{9,8},{10,11... | collective-permute-start | bytes 344072 | tf_op jit(solution)/shard_map/ppermute | solution.py:1001
where the time goes:
time: 105 us; the launch traced here: 106 us
  waiting for transfers between devices  38.9 us (37%)
  starting transfers between devices  37.3 us (36%)
  Pallas kernels  24.4 us (23%)
  local copies, waits for them, and re-layouts  4.06 us (4%)
  between operations  1.49 us (1%)
    ppermute x7, starting transfers between devices, to_fragment(): lax.ppermute(block, 'orb', [(i, (i + distance) % devices) for i in senders])  24.3 us
    ppermute x7, waiting for transfers between devices, to_fragment(): lax.ppermute(block, 'orb', [(i, (i + distance) % devices) for i in senders])  23.2 us
    pallas_call x2, Pallas kernels, pair_terms(): pl.pallas_call(functools.partial(pair_kernel, shape, second_part), out_sh...  12.9 us
    ppermute x13, waiting for transfers between devices, with_member(): lax.ppermute(block, 'grp', [(i, i ^ bit) for i in range(lax.axis_size('gr...  8.29 us
    ppermute x2, waiting for transfers between devices, with_twin(): lax.ppermute(block, 'orb', [(i, i ^ 1) for i in range(lax.axis_size('orb'...  7.4 us
    ppermute x2, starting transfers between devices, with_twin(): lax.ppermute(block, 'orb', [(i, i ^ 1) for i in range(lax.axis_size('orb'...  6.76 us
    ppermute x13, starting transfers between devices, with_member(): lax.ppermute(block, 'grp', [(i, i ^ bit) for i in range(lax.axis_size('gr...  6.27 us
    pallas_call x1, Pallas kernels, screen_terms(): pl.pallas_call(functools.partial(screen_kernel, edge), out_shape=[jax.Sha...  3.54 us
  transfers between devices with their start and end apart: 22, of which 10 were waited for; matrix products, arithmetic and copies ran while one was open for 3% of the time, Pallas kernels for 20%

commit v1 on v0

--- a/solution.py
+++ b/solution.py
@@ -1038,6 +1038,7 @@
     tables = [screen, *tables]
     sizes = (anchors.shape[0], pair_first.shape[0])
     act, two_tail, two_head, back = pair_terms(numbers, *sizes, tables, pieces, [twin, two])
+    two_tail, relay, one = together(two_tail, relay, one)
     two_tail = to_fragment(two_tail, 2)
     kept, sent, one_head, one_tail, own = pair_terms(
         numbers, *sizes, tables, pieces, [twin, relay, one], [act, back]

time: 105 us -> 107 us (1.019); the launches traced: 106 us -> 106 us
  starting transfers between devices: 37.3 us -> 24.8 us
  waiting for transfers between devices: 38.9 us -> 51 us
    ppermute x7, starting transfers between devices: 24.3 us -> 13.2 us  [to_fragment(): lax.ppermute(block, 'orb', [(i, (i + distance) % devices) for i in senders])]
    ppermute x7, waiting for transfers between devices: 23.2 us -> 28.5 us  [to_fragment(): lax.ppermute(block, 'orb', [(i, (i + distance) % devices) for i in senders])]
    ppermute x2, waiting for transfers between devices: 7.4 us -> 11.6 us  [with_twin(): lax.ppermute(block, 'orb', [(i, i ^ 1) for i in range(lax.axis_size('orb'...]
    ppermute x2, starting transfers between devices: 6.76 us -> 3.81 us  [with_twin(): lax.ppermute(block, 'orb', [(i, i ^ 1) for i in range(lax.axis_size('orb'...]
    ppermute x13, waiting for transfers between devices: 8.29 us -> 10.9 us  [with_member(): lax.ppermute(block, 'grp', [(i, i ^ bit) for i in range(lax.axis_size('gr...]
    ppermute x13, starting transfers between devices: 6.27 us -> 7.81 us  [with_member(): lax.ppermute(block, 'grp', [(i, i ^ bit) for i in range(lax.axis_size('gr...]
  transfers between devices with their start and end apart: 22 -> 22, of which waited for: 10 -> 12; matrix products, arithmetic and copies ran while one was open for 3% -> 3% of each run, Pallas kernels for 20% -> 21%
where the time goes in v1:
time: 107 us; the launch traced here: 106 us
  waiting for transfers between devices  51 us (48%)
  starting transfers between devices  24.8 us (23%)
  Pallas kernels  24.7 us (23%)
  local copies, waits for them, and re-layouts  4.06 us (4%)
  between operations  1.46 us (1%)
    ppermute x7, waiting for transfers between devices, to_fragment(): lax.ppermute(block, 'orb', [(i, (i + distance) % devices) for i in senders])  28.5 us
    pallas_call x2, Pallas kernels, pair_terms(): pl.pallas_call(functools.partial(pair_kernel, shape, second_part), out_sh...  13.2 us
    ppermute x7, starting transfers between devices, to_fragment(): lax.ppermute(block, 'orb', [(i, (i + distance) % devices) for i in senders])  13.2 us
    ppermute x2, waiting for transfers between devices, with_twin(): lax.ppermute(block, 'orb', [(i, i ^ 1) for i in range(lax.axis_size('orb'...  11.6 us
    ppermute x13, waiting for transfers between devices, with_member(): lax.ppermute(block, 'grp', [(i, i ^ bit) for i in range(lax.axis_size('gr...  10.9 us
    ppermute x13, starting transfers between devices, with_member(): lax.ppermute(block, 'grp', [(i, i ^ bit) for i in range(lax.axis_size('gr...  7.81 us
    ppermute x2, starting transfers between devices, with_twin(): lax.ppermute(block, 'orb', [(i, i ^ 1) for i in range(lax.axis_size('orb'...  3.81 us
    pallas_call x1, Pallas kernels, screen_terms(): pl.pallas_call(functools.partial(screen_kernel, edge), out_shape=[jax.Sha...  3.54 us
  transfers between devices with their start and end apart: 22, of which 12 were waited for; matrix products, arithmetic and copies ran while one was open for 3% of the time, Pallas kernels for 21%

profile of v1, /device:TPU:0, one launch (start us, length us, event | category | flops | bytes accessed | tf_op | source)
XLA Modules:
  0.0 106.3 jit_solution(12430287431917905108)
XLA Ops:
  0.7 5.1 %collective-permute-start.1 = (f32[2,48,2304]{2,1,0:T(8,128)}, f32[2,48,2304]{2,1,0:T(8,128)}, u32[]{:S(2)}, u32[]{:S(2)}) collective-permute-start(f32[2,48,2304]{2,1,0:T(8,128)} %refs_3_.3), channel_id=1, source_target_pairs={{0,24},{4,28},{8,0},{12,4},{16,8},{20,12},{24,16},{28,20},{1,25},{... | collective-permute-start | bytes 2654216 | tf_op jit(solution)/shard_map/ppermute | solution.py:993
  5.8 1.5 %collective-permute-start.3 = (f32[2,48,2304]{2,1,0:T(8,128)}, f32[2,48,2304]{2,1,0:T(8,128)S(1)}, u32[]{:S(2)}, u32[]{:S(2)}) collective-permute-start(f32[2,48,2304]{2,1,0:T(8,128)} %refs_3_.3), channel_id=1, source_target_pairs={{0,2},{1,3},{2,0},{3,1},{4,6},{5,7},{6,4},{7,5},{8,10},{9,11},{10,... | collective-permute-start | bytes 2654216 | tf_op jit(solution)/shard_map/ppermute | solution.py:1001
  7.3 2.1 %fusion.1 = (f32[1,48,2304]{2,1,0:T(8,128)}, f32[1,48,2304]{2,1,0:T(8,128)}) fusion(f32[2,48,2304]{2,1,0:T(8,128)} %refs_3_.3), kind=kLoop, calls=%fused_computation.2 | loop fusion | bytes 1769472 | tf_op jit(solution)/shard_map/slice | solution.py:1032
  9.4 1.5 %collective-permute-start.2 = (f32[1,48,2304]{2,1,0:T(8,128)}, f32[1,48,2304]{2,1,0:T(8,128)S(1)}, u32[]{:S(2)}, u32[]{:S(2)}) collective-permute-start(f32[1,48,2304]{2,1,0:T(8,128)} %get-tuple-element.93), channel_id=1, source_target_pairs={{0,4},{4,0},{8,12},{12,8},{16,20},{20,16},{24,28},{28,24},{1,5},{5... | collective-permute-start | bytes 1327112 | tf_op jit(solution)/shard_map/ppermute | solution.py:997
  12.5 0.9 copy-done.2
  13.4 3.5 %screen_terms.1 = (f32[1536,128]{1,0:T(8,128)S(1)}, s32[51]{0:T(128)S(1)}, bf16[768,256]{1,0:T(8,128)(2,1)S(1)}, bf16[768,256]{1,0:T(8,128)(2,1)S(1)}) custom-call(s32[51]{0:T(128)S(1)} %concatenate.4.numbers_ref, f32[48,2304]{1,0:T(8,128)S(1)} %copy-done.1, bf16[2,2,128,128]{3,2,1,0:T(8,128)(2,1)S(1)} %copy-done.2), custom_call_target="tpu_custom_call" | custom-call | tf_op jit(solution)/shard_map/screen_terms/pallas_call | solution.py:304
  17.0 4.0 %collective-permute-done.2.refs_7_ = f32[1,48,2304]{2,1,0:T(8,128)S(1)} collective-permute-done((f32[1,48,2304]{2,1,0:T(8,128)}, f32[1,48,2304]{2,1,0:T(8,128)S(1)}, u32[]{:S(2)}, u32[]{:S(2)}) %collective-permute-start.2) | collective-permute-done | bytes 442400 | tf_op jit(solution)/shard_map/ppermute | solution.py:997
  21.0 4.0 %collective-permute-done.1.refs_8_ = f32[2,48,2304]{2,1,0:T(8,128)} collective-permute-done((f32[2,48,2304]{2,1,0:T(8,128)}, f32[2,48,2304]{2,1,0:T(8,128)}, u32[]{:S(2)}, u32[]{:S(2)}) %collective-permute-start.1) | collective-permute-done | bytes 884768 | tf_op jit(solution)/shard_map/ppermute | solution.py:993
  25.0 2.1 %collective-permute-done.3.refs_2_.refs_5_ = f32[2,48,2304]{2,1,0:T(8,128)S(1)} collective-permute-done((f32[2,48,2304]{2,1,0:T(8,128)}, f32[2,48,2304]{2,1,0:T(8,128)S(1)}, u32[]{:S(2)}, u32[]{:S(2)}) %collective-permute-start.3) | collective-permute-done | bytes 884768 | tf_op jit(solution)/shard_map/ppermute | solution.py:1001
  27.8 4.4 %collective-permute-start.6 = (f32[1,48,2304]{2,1,0:T(8,128)}, f32[1,48,2304]{2,1,0:T(8,128)S(1)}, u32[]{:S(2)}, u32[]{:S(2)}) collective-permute-start(f32[1,48,2304]{2,1,0:T(8,128)} %get-tuple-element.59), channel_id=1, source_target_pairs={{0,28},{4,0},{8,4},{12,8},{16,12},{20,16},{24,20},{28,24},{1,29},{... | collective-permute-start | bytes 1327112 | tf_op jit(solution)/shard_map/ppermute | solution.py:993
  32.2 10.1 %early_pair_terms.1 = (f32[8,864,128]{2,1,0:T(8,128)S(1)}, f32[1,864,128]{2,1,0:T(8,128)S(1)}, f32[1,864,128]{2,1,0:T(8,128)S(1)}, f32[4,864,128]{2,1,0:T(8,128)S(1)}) custom-call(s32[51]{0:T(128)S(1)} %get-tuple-element.52.numbers_ref, f32[1536,128]{1,0:T(8,128)S(1)} %get-tuple-element.53.refs_0_, bf16[768,256]{1,0:T(8,128)(2,1)S(1)} %get-tuple-element.54.refs_1_, ...), custom_call_target="tpu_custom_call" | custom-call | tf_op jit(solution)/shard_map/early_pair_terms/pallas_call | solution.py:737
  42.3 1.2 %collective-permute-done.6.refs_9_ = f32[1,48,2304]{2,1,0:T(8,128)S(1)} collective-permute-done((f32[1,48,2304]{2,1,0:T(8,128)}, f32[1,48,2304]{2,1,0:T(8,128)S(1)}, u32[]{:S(2)}, u32[]{:S(2)}) %collective-permute-start.6) | collective-permute-done | bytes 442400 | tf_op jit(solution)/shard_map/ppermute | solution.py:993
  43.5 0.8 collective-permute-start.7
  44.3 3.1 %late_pair_terms.1 = (f32[2,8,216,128]{3,2,1,0:T(8,128)S(1)}, f32[2,8,216,128]{3,2,1,0:T(8,128)S(1)}, f32[1,864,128]{2,1,0:T(8,128)S(1)}, f32[1,864,128]{2,1,0:T(8,128)S(1)}, f32[2,864,128]{2,1,0:T(8,128)S(1)}) custom-call(s32[51]{0:T(128)S(1)} %get-tuple-element.52.numbers_ref, f32[1536,128]{1,0:T(8,128)S(1)} %get-tuple-element.53.refs_0_, ...), custom_call_target="tpu_custom_call" | custom-call | tf_op jit(solution)/shard_map/late_pair_terms/pallas_call | solution.py:737
  47.5 9.7 %collective-permute-done.7.refs_0_ = f32[1,864,128]{2,1,0:T(8,128)S(1)} collective-permute-done((f32[1,864,128]{2,1,0:T(8,128)S(1)}, f32[1,864,128]{2,1,0:T(8,128)S(1)}, u32[]{:S(2)}, u32[]{:S(2)}) %collective-permute-start.7) | collective-permute-done | bytes 442400 | tf_op jit(solution)/shard_map/ppermute | solution.py:993
  57.1 2.3 %collective-permute-start.10 = (f32[1,864,128]{2,1,0:T(8,128)S(1)}, f32[1,864,128]{2,1,0:T(8,128)S(1)}, u32[]{:S(2)}, u32[]{:S(2)}) collective-permute-start(f32[1,864,128]{2,1,0:T(8,128)S(1)} %get-tuple-element.72), channel_id=1, source_target_pairs={{0,4},{4,0},{8,12},{12,8},{16,20},{20,16},{24,28},{28,24},{1,5},{5... | collective-permute-start | bytes 1327112 | tf_op jit(solution)/shard_map/ppermute | solution.py:997
  59.4 1.4 %collective-permute-done.8 = f32[2,8,216,128]{3,2,1,0:T(8,128)S(1)} collective-permute-done((f32[2,8,216,128]{3,2,1,0:T(8,128)S(1)}, f32[2,8,216,128]{3,2,1,0:T(8,128)S(1)}, u32[]{:S(2)}, u32[]{:S(2)}) %collective-permute-start.8) | collective-permute-done | bytes 1769504 | tf_op jit(solution)/shard_map/ppermute | solution.py:1001
  61.1 1.6 %collective-permute-start.9 = (f32[1,8,216,128]{3,2,1,0:T(8,128)S(1)}, f32[1,8,216,128]{3,2,1,0:T(8,128)S(1)}, u32[]{:S(2)}, u32[]{:S(2)}) collective-permute-start(f32[1,8,216,128]{3,2,1,0:T(8,128)S(1)} %get-tuple-element.90), channel_id=1, source_target_pairs={{0,2},{1,3},{2,0},{3,1},{4,6},{5,7},{6,4},{7,5},{8,10},{9,11},{10,... | collective-permute-start | bytes 2654216 | tf_op jit(solution)/shard_map/ppermute | solution.py:1001
  62.7 7.6 %collective-permute-done.10.refs_1_ = f32[1,864,128]{2,1,0:T(8,128)S(1)} collective-permute-done((f32[1,864,128]{2,1,0:T(8,128)S(1)}, f32[1,864,128]{2,1,0:T(8,128)S(1)}, u32[]{:S(2)}, u32[]{:S(2)}) %collective-permute-start.10) | collective-permute-done | bytes 442400 | tf_op jit(solution)/shard_map/ppermute | solution.py:997
  70.3 3.3 %collective-permute-done.11.refs_0_ = f32[1,864,128]{2,1,0:T(8,128)S(1)} collective-permute-done((f32[1,864,128]{2,1,0:T(8,128)S(1)}, f32[1,864,128]{2,1,0:T(8,128)S(1)}, u32[]{:S(2)}, u32[]{:S(2)}) %collective-permute-start.11) | collective-permute-done | bytes 442400 | tf_op jit(solution)/shard_map/ppermute | solution.py:993
  73.8 1.9 %collective-permute-start.12 = (f32[1,864,128]{2,1,0:T(8,128)S(1)}, f32[1,864,128]{2,1,0:T(8,128)S(1)}, u32[]{:S(2)}, u32[]{:S(2)}) collective-permute-start(f32[1,864,128]{2,1,0:T(8,128)S(1)} %collective-permute-done.10.refs_1_), channel_id=1, source_target_pairs={{0,8},{8,16},{16,24},{24,0},{1,9},{9,17},{17,25},{25,1},{2,10},{10... | collective-permute-start | bytes 1327112 | tf_op jit(solution)/shard_map/ppermute | solution.py:993
  75.8 1.5 %flatten_terms.1 = (f32[8,864,128]{2,1,0:T(8,128)S(1)}, f32[8,216,128]{2,1,0:T(8,128)S(1)}) custom-call(s32[2]{0:T(128)S(1)} %pad_add_fusion.places_ref, f32[2,48,2304]{2,1,0:T(8,128)S(1)} %copy-done, f32[2,48,2304]{2,1,0:T(8,128)S(1)} %collective-permute-done.refs_1_.refs_4_, f32[2,48,2304]{2,1,0:T(8,128)S(1)} %collective-permute-done.3.refs_2_.refs_5_, ...), custom_call_target="tpu_custom_call" | custom-call | tf_op jit(solution)/shard_map/flatten_terms/pallas_call | solution.py:788
  77.3 10.4 %collective-permute-done.17.refs_1_ = f32[1,864,128]{2,1,0:T(8,128)S(1)} collective-permute-done((f32[1,864,128]{2,1,0:T(8,128)S(1)}, f32[1,864,128]{2,1,0:T(8,128)S(1)}, u32[]{:S(2)}, u32[]{:S(2)}) %collective-permute-start.17) | collective-permute-done | bytes 442400 | tf_op jit(solution)/shard_map/ppermute | solution.py:993
  87.7 1.1 %home_terms.3 = (f32[224,128]{1,0:T(8,128)S(1)}, f32[224,128]{1,0:T(8,128)S(1)}, f32[224,128]{1,0:T(8,128)S(1)}, f32[224,128]{1,0:T(8,128)S(1)}) custom-call(s32[2]{0:T(128)S(1)} %pad_add_fusion.places_ref, f32[8,864,128]{2,1,0:T(8,128)S(1)} %get-tuple-element.70.flat_ref, f32[2,864,128]{2,1,0:T(8,128)S(1)} %get-tuple-element.71.own_ref, ...), custom_call_target="tpu_custom_call" | custom-call | tf_op jit(solution)/shard_map/home_terms/pallas_call | solution.py:909
  88.8 1.6 %collective-permute-start.20 = (f32[224,128]{1,0:T(8,128)S(1)}, f32[224,128]{1,0:T(8,128)S(1)}, u32[]{:S(2)}, u32[]{:S(2)}) collective-permute-start(f32[224,128]{1,0:T(8,128)S(1)} %get-tuple-element.87), channel_id=1, source_target_pairs={{0,2},{1,3},{2,0},{3,1},{4,6},{5,7},{6,4},{7,5},{8,10},{9,11},{10,... | collective-permute-start | bytes 344072 | tf_op jit(solution)/shard_map/ppermute | solution.py:1001
  90.4 1.6 %action_terms.1 = (f32[8,216,128]{2,1,0:T(8,128)S(1)}, f32[8,128]{1,0:T(8,128)S(1)}) custom-call(s32[2]{0:T(128)S(1)} %pad_add_fusion.places_ref, f32[8,216,128]{2,1,0:T(8,128)S(1)} %get-tuple-element.51.phi_ref, f32[1,8,216,128]{3,2,1,0:T(8,128)S(1)} %get-tuple-element.91.kept_ref, f32[1,8,216,128]{3,2,1,0:T(8,128)S(1)} %collective-permute-done.9.refs_0_), custom_call_target="tpu_custom_call" | custom-call | tf_op jit(solution)/shard_map/action_terms/pallas_call | solution.py:853
  92.0 1.1 %home_terms.2 = (f32[224,128]{1,0:T(8,128)S(1)}, f32[224,128]{1,0:T(8,128)S(1)}, f32[224,128]{1,0:T(8,128)S(1)}, f32[224,128]{1,0:T(8,128)S(1)}) custom-call(s32[2]{0:T(128)S(1)} %pad_add_fusion.places_ref, f32[8,864,128]{2,1,0:T(8,128)S(1)} %get-tuple-element.70.flat_ref, f32[2,864,128]{2,1,0:T(8,128)S(1)} %get-tuple-element.71.own_ref, ...), custom_call_target="tpu_custom_call" | custom-call | tf_op jit(solution)/shard_map/home_terms/pallas_call | solution.py:909
  93.7 1.5 %collective-permute-start.19 = (f32[224,128]{1,0:T(8,128)S(1)}, f32[224,128]{1,0:T(8,128)S(1)}, u32[]{:S(2)}, u32[]{:S(2)}) collective-permute-start(f32[224,128]{1,0:T(8,128)S(1)} %get-tuple-element.86), channel_id=1, source_target_pairs={{0,2},{1,3},{2,0},{3,1},{4,6},{5,7},{6,4},{7,5},{8,10},{9,11},{10,... | collective-permute-start | bytes 344072 | tf_op jit(solution)/shard_map/ppermute | solution.py:1001
  96.2 2.9 %collective-permute-done.15 = f32[224,128]{1,0:T(8,128)S(1)} collective-permute-done((f32[224,128]{1,0:T(8,128)S(1)}, f32[224,128]{1,0:T(8,128)S(1)}, u32[]{:S(2)}, u32[]{:S(2)}) %collective-permute-start.15) | collective-permute-done | bytes 114720 | tf_op jit(solution)/shard_map/ppermute | solution.py:1001
  99.1 2.5 %collective-permute-done.19.refs_6_ = f32[224,128]{1,0:T(8,128)S(1)} collective-permute-done((f32[224,128]{1,0:T(8,128)S(1)}, f32[224,128]{1,0:T(8,128)S(1)}, u32[]{:S(2)}, u32[]{:S(2)}) %collective-permute-start.19) | collective-permute-done | bytes 114720 | tf_op jit(solution)/shard_map/ppermute | solution.py:1001
  101.6 2.1 %collective-permute-done.14.refs_2_ = f32[224,128]{1,0:T(8,128)S(1)} collective-permute-done((f32[224,128]{1,0:T(8,128)S(1)}, f32[224,128]{1,0:T(8,128)S(1)}, u32[]{:S(2)}, u32[]{:S(2)}) %collective-permute-start.14) | collective-permute-done | bytes 114720 | tf_op jit(solution)/shard_map/ppermute | solution.py:1001
  103.7 2.7 %gradient_terms.1 = (f32[12,8,2304]{2,1,0:T(8,128)}, f32[8,8]{1,0:T(8,128)}) custom-call(s32[2]{0:T(128)S(1)} %pad_add_fusion.places_ref, f32[8,216,128]{2,1,0:T(8,128)S(1)} %get-tuple-element.69.act_ref, f32[8,216,128]{2,1,0:T(8,128)S(1)} %get-tuple-element.51.phi_ref, f32[224,128]{1,0:T(8,128)S(1)} %get-tuple-element.78.refs_0_, ...), custom_call_target="tpu_custom_call" | custom-call | tf_op jit(solution)/shard_map/gradient_terms/pallas_call | solution.py:971
  (39 shorter events, 3.9 us)
Async XLA Ops:
  0.6 10.3 %copy-start = (f32[2,48,2304]{2,1,0:T(8,128)S(1)}, f32[2,48,2304]{2,1,0:T(8,128)}, u32[]{:S(2)}) copy-start(f32[2,48,2304]{2,1,0:T(8,128)} %refs_3_.3) | copy-start | bytes 2654212
  0.6 10.3 %copy-start.3 = (s32[8,3]{0,1:T(4,128)S(1)}, s32[8,3]{0,1:T(4,128)}, u32[]{:S(2)}) copy-start(s32[8,3]{0,1:T(4,128)} %param.10) | copy-start | bytes 292
  0.7 11.1 %copy-start.4 = (s32[8]{0:T(128)S(1)}, s32[8]{0:T(128)}, u32[]{:S(2)}) copy-start(s32[8]{0:T(128)} %param.12) | copy-start | bytes 100
  0.7 11.1 %copy-start.5 = (s32[8]{0:T(128)S(1)}, s32[8]{0:T(128)}, u32[]{:S(2)}) copy-start(s32[8]{0:T(128)} %param.13) | copy-start | bytes 100
  0.7 11.8 %copy-start.1 = (f32[48,2304]{1,0:T(8,128)S(1)}, f32[48,2304]{1,0:T(8,128)}, u32[]{:S(2)}) copy-start(f32[48,2304]{1,0:T(8,128)} %kernel_ref.1) | copy-start | bytes 1327108
  0.7 24.3 %collective-permute-start.1 = (f32[2,48,2304]{2,1,0:T(8,128)}, f32[2,48,2304]{2,1,0:T(8,128)}, u32[]{:S(2)}, u32[]{:S(2)}) collective-permute-start(f32[2,48,2304]{2,1,0:T(8,128)} %refs_3_.3), channel_id=1, source_target_pairs={{0,24},{4,28},{8,0},{12,4},{16,8},{20,12},{24,16},{28,20},{1,25},{... | collective-permute-start | bytes 2654216 | tf_op jit(solution)/shard_map/ppermute | solution.py:993
  5.8 21.3 %collective-permute-start.3 = (f32[2,48,2304]{2,1,0:T(8,128)}, f32[2,48,2304]{2,1,0:T(8,128)S(1)}, u32[]{:S(2)}, u32[]{:S(2)}) collective-permute-start(f32[2,48,2304]{2,1,0:T(8,128)} %refs_3_.3), channel_id=1, source_target_pairs={{0,2},{1,3},{2,0},{3,1},{4,6},{5,7},{6,4},{7,5},{8,10},{9,11},{10,... | collective-permute-start | bytes 2654216 | tf_op jit(solution)/shard_map/ppermute | solution.py:1001
  9.4 11.6 %collective-permute-start.2 = (f32[1,48,2304]{2,1,0:T(8,128)}, f32[1,48,2304]{2,1,0:T(8,128)S(1)}, u32[]{:S(2)}, u32[]{:S(2)}) collective-permute-start(f32[1,48,2304]{2,1,0:T(8,128)} %get-tuple-element.93), channel_id=1, source_target_pairs={{0,4},{4,0},{8,12},{12,8},{16,20},{20,16},{24,28},{28,24},{1,5},{5... | collective-permute-start | bytes 1327112 | tf_op jit(solution)/shard_map/ppermute | solution.py:997
  10.9 21.3 %collective-permute-start = (f32[2,48,2304]{2,1,0:T(8,128)S(1)}, f32[2,48,2304]{2,1,0:T(8,128)S(1)}, u32[]{:S(2)}, u32[]{:S(2)}) collective-permute-start(f32[2,48,2304]{2,1,0:T(8,128)S(1)} %copy-done), channel_id=1, source_target_pairs={{0,1},{1,0},{2,3},{3,2},{4,5},{5,4},{6,7},{7,6},{8,9},{9,8},{10,11... | collective-permute-start | bytes 2654216 | tf_op jit(solution)/shard_map/ppermute | solution.py:1001
  12.5 0.9 copy-start.2
  27.1 5.1 %collective-permute-start.4 = (f32[2,48,2304]{2,1,0:T(8,128)S(1)}, f32[2,48,2304]{2,1,0:T(8,128)S(1)}, u32[]{:S(2)}, u32[]{:S(2)}) collective-permute-start(f32[2,48,2304]{2,1,0:T(8,128)S(1)} %collective-permute-done.3.refs_2_.refs_5_), channel_id=1, source_target_pairs={{0,1},{1,0},{2,3},{3,2},{4,5},{5,4},{6,7},{7,6},{8,9},{9,8},{10,11... | collective-permute-start | bytes 2654216 | tf_op jit(solution)/shard_map/ppermute | solution.py:1001
  27.1 15.2 %collective-permute-start.5 = (f32[1,48,2304]{2,1,0:T(8,128)S(1)}, f32[1,48,2304]{2,1,0:T(8,128)S(1)}, u32[]{:S(2)}, u32[]{:S(2)}) collective-permute-start(f32[1,48,2304]{2,1,0:T(8,128)S(1)} %collective-permute-done.2.refs_7_), channel_id=1, source_target_pairs={{4,28},{12,4},{20,12},{28,20},{5,29},{13,5},{21,13},{29,21},{6,30}... | collective-permute-start | bytes 1327112 | tf_op jit(solution)/shard_map/ppermute | solution.py:993
  27.8 15.7 %collective-permute-start.6 = (f32[1,48,2304]{2,1,0:T(8,128)}, f32[1,48,2304]{2,1,0:T(8,128)S(1)}, u32[]{:S(2)}, u32[]{:S(2)}) collective-permute-start(f32[1,48,2304]{2,1,0:T(8,128)} %get-tuple-element.59), channel_id=1, source_target_pairs={{0,28},{4,0},{8,4},{12,8},{16,12},{20,16},{24,20},{28,24},{1,29},{... | collective-permute-start | bytes 1327112 | tf_op jit(solution)/shard_map/ppermute | solution.py:993
  43.5 13.6 %collective-permute-start.7 = (f32[1,864,128]{2,1,0:T(8,128)S(1)}, f32[1,864,128]{2,1,0:T(8,128)S(1)}, u32[]{:S(2)}, u32[]{:S(2)}) collective-permute-start(f32[1,864,128]{2,1,0:T(8,128)S(1)} %get-tuple-element.66), channel_id=1, source_target_pairs={{0,8},{4,12},{8,16},{12,20},{16,24},{20,28},{24,0},{28,4},{1,9},{5... | collective-permute-start | bytes 1327112 | tf_op jit(solution)/shard_map/ppermute | solution.py:993
  57.1 3.7 %collective-permute-start.8 = (f32[2,8,216,128]{3,2,1,0:T(8,128)S(1)}, f32[2,8,216,128]{3,2,1,0:T(8,128)S(1)}, u32[]{:S(2)}, u32[]{:S(2)}) collective-permute-start(f32[2,8,216,128]{3,2,1,0:T(8,128)S(1)} %get-tuple-element.68), channel_id=1, source_target_pairs={{0,1},{1,0},{2,3},{3,2},{4,5},{5,4},{6,7},{7,6},{8,9},{9,8},{10,11... | collective-permute-start | bytes 5308424 | tf_op jit(solution)/shard_map/ppermute | solution.py:1001
  57.1 13.2 %collective-permute-start.10 = (f32[1,864,128]{2,1,0:T(8,128)S(1)}, f32[1,864,128]{2,1,0:T(8,128)S(1)}, u32[]{:S(2)}, u32[]{:S(2)}) collective-permute-start(f32[1,864,128]{2,1,0:T(8,128)S(1)} %get-tuple-element.72), channel_id=1, source_target_pairs={{0,4},{4,0},{8,12},{12,8},{16,20},{20,16},{24,28},{28,24},{1,5},{5... | collective-permute-start | bytes 1327112 | tf_op jit(solution)/shard_map/ppermute | solution.py:997
  59.4 14.1 %collective-permute-start.11 = (f32[1,864,128]{2,1,0:T(8,128)S(1)}, f32[1,864,128]{2,1,0:T(8,128)S(1)}, u32[]{:S(2)}, u32[]{:S(2)}) collective-permute-start(f32[1,864,128]{2,1,0:T(8,128)S(1)} %get-tuple-element.74), channel_id=1, source_target_pairs={{0,8},{4,12},{8,16},{12,20},{16,24},{20,28},{24,0},{28,4},{1,9},{5... | collective-permute-start | bytes 1327112 | tf_op jit(solution)/shard_map/ppermute | solution.py:993
  61.1 29.3 %collective-permute-start.9 = (f32[1,8,216,128]{3,2,1,0:T(8,128)S(1)}, f32[1,8,216,128]{3,2,1,0:T(8,128)S(1)}, u32[]{:S(2)}, u32[]{:S(2)}) collective-permute-start(f32[1,8,216,128]{3,2,1,0:T(8,128)S(1)} %get-tuple-element.90), channel_id=1, source_target_pairs={{0,2},{1,3},{2,0},{3,1},{4,6},{5,7},{6,4},{7,5},{8,10},{9,11},{10,... | collective-permute-start | bytes 2654216 | tf_op jit(solution)/shard_map/ppermute | solution.py:1001
  73.5 14.2 %collective-permute-start.17 = (f32[1,864,128]{2,1,0:T(8,128)S(1)}, f32[1,864,128]{2,1,0:T(8,128)S(1)}, u32[]{:S(2)}, u32[]{:S(2)}) collective-permute-start(f32[1,864,128]{2,1,0:T(8,128)S(1)} %get-tuple-element.83), channel_id=1, source_target_pairs={{0,4},{4,8},{8,12},{12,16},{16,20},{20,24},{24,28},{28,0},{1,5},{5... | collective-permute-start | bytes 1327112 | tf_op jit(solution)/shard_map/ppermute | solution.py:993
  73.8 18.2 %collective-permute-start.12 = (f32[1,864,128]{2,1,0:T(8,128)S(1)}, f32[1,864,128]{2,1,0:T(8,128)S(1)}, u32[]{:S(2)}, u32[]{:S(2)}) collective-permute-start(f32[1,864,128]{2,1,0:T(8,128)S(1)} %collective-permute-done.10.refs_1_), channel_id=1, source_target_pairs={{0,8},{8,16},{16,24},{24,0},{1,9},{9,17},{17,25},{25,1},{2,10},{10... | collective-permute-start | bytes 1327112 | tf_op jit(solution)/shard_map/ppermute | solution.py:993
  88.8 6.4 %collective-permute-start.20 = (f32[224,128]{1,0:T(8,128)S(1)}, f32[224,128]{1,0:T(8,128)S(1)}, u32[]{:S(2)}, u32[]{:S(2)}) collective-permute-start(f32[224,128]{1,0:T(8,128)S(1)} %get-tuple-element.87), channel_id=1, source_target_pairs={{0,2},{1,3},{2,0},{3,1},{4,6},{5,7},{6,4},{7,5},{8,10},{9,11},{10,... | collective-permute-start | bytes 344072 | tf_op jit(solution)/shard_map/ppermute | solution.py:1001
  90.4 5.3 %collective-permute-start.18 = (f32[224,128]{1,0:T(8,128)S(1)}, f32[224,128]{1,0:T(8,128)S(1)}, u32[]{:S(2)}, u32[]{:S(2)}) collective-permute-start(f32[224,128]{1,0:T(8,128)S(1)} %get-tuple-element.85), channel_id=1, source_target_pairs={{0,1},{1,0},{2,3},{3,2},{4,5},{5,4},{6,7},{7,6},{8,9},{9,8},{10,11... | collective-permute-start | bytes 344072 | tf_op jit(solution)/shard_map/ppermute | solution.py:1001
  93.1 6.0 %collective-permute-start.15 = (f32[224,128]{1,0:T(8,128)S(1)}, f32[224,128]{1,0:T(8,128)S(1)}, u32[]{:S(2)}, u32[]{:S(2)}) collective-permute-start(f32[224,128]{1,0:T(8,128)S(1)} %get-tuple-element.81), channel_id=1, source_target_pairs={{0,2},{1,3},{2,0},{3,1},{4,6},{5,7},{6,4},{7,5},{8,10},{9,11},{10,... | collective-permute-start | bytes 344072 | tf_op jit(solution)/shard_map/ppermute | solution.py:1001
  93.7 7.9 %collective-permute-start.19 = (f32[224,128]{1,0:T(8,128)S(1)}, f32[224,128]{1,0:T(8,128)S(1)}, u32[]{:S(2)}, u32[]{:S(2)}) collective-permute-start(f32[224,128]{1,0:T(8,128)S(1)} %get-tuple-element.86), channel_id=1, source_target_pairs={{0,2},{1,3},{2,0},{3,1},{4,6},{5,7},{6,4},{7,5},{8,10},{9,11},{10,... | collective-permute-start | bytes 344072 | tf_op jit(solution)/shard_map/ppermute | solution.py:1001
  95.2 6.4 %collective-permute-start.21 = (f32[224,128]{1,0:T(8,128)S(1)}, f32[224,128]{1,0:T(8,128)S(1)}, u32[]{:S(2)}, u32[]{:S(2)}) collective-permute-start(f32[224,128]{1,0:T(8,128)S(1)} %collective-permute-done.20), channel_id=1, source_target_pairs={{0,1},{1,0},{2,3},{3,2},{4,5},{5,4},{6,7},{7,6},{8,9},{9,8},{10,11... | collective-permute-start | bytes 344072 | tf_op jit(solution)/shard_map/ppermute | solution.py:1001
  95.2 6.4 %collective-permute-start.13 = (f32[224,128]{1,0:T(8,128)S(1)}, f32[224,128]{1,0:T(8,128)S(1)}, u32[]{:S(2)}, u32[]{:S(2)}) collective-permute-start(f32[224,128]{1,0:T(8,128)S(1)} %get-tuple-element.79), channel_id=1, source_target_pairs={{0,1},{1,0},{2,3},{3,2},{4,5},{5,4},{6,7},{7,6},{8,9},{9,8},{10,11... | collective-permute-start | bytes 344072 | tf_op jit(solution)/shard_map/ppermute | solution.py:1001
  95.7 7.9 %collective-permute-start.14 = (f32[224,128]{1,0:T(8,128)S(1)}, f32[224,128]{1,0:T(8,128)S(1)}, u32[]{:S(2)}, u32[]{:S(2)}) collective-permute-start(f32[224,128]{1,0:T(8,128)S(1)} %get-tuple-element.80), channel_id=1, source_target_pairs={{0,2},{1,3},{2,0},{3,1},{4,6},{5,7},{6,4},{7,5},{8,10},{9,11},{10,... | collective-permute-start | bytes 344072 | tf_op jit(solution)/shard_map/ppermute | solution.py:1001
  99.1 4.5 %collective-permute-start.16 = (f32[224,128]{1,0:T(8,128)S(1)}, f32[224,128]{1,0:T(8,128)S(1)}, u32[]{:S(2)}, u32[]{:S(2)}) collective-permute-start(f32[224,128]{1,0:T(8,128)S(1)} %collective-permute-done.15), channel_id=1, source_target_pairs={{0,1},{1,0},{2,3},{3,2},{4,5},{5,4},{6,7},{7,6},{8,9},{9,8},{10,11... | collective-permute-start | bytes 344072 | tf_op jit(solution)/shard_map/ppermute | solution.py:1001

commit v2 on v1

--- a/solution.py
+++ b/solution.py
@@ -328,7 +328,7 @@
     phi_refs, refs = refs[:groups], refs[groups:]
     if second_part:
         (twin_ref, relay_ref, one_ref, act_before, back_before), refs = refs[:5], refs[5:]
-        act_outs, back_outs, refs = refs[:2], refs[2:5], refs[5:]
+        act_outs, back_outs, refs = refs[:groups], refs[groups : groups + 3], refs[groups + 3 :]
         (act, back, state_sem, out_sem), refs = refs[:4], refs[4:]
     else:
         (twin_ref, two_ref, act), back_outs, refs = refs[:3], refs[3:6], refs[6:]
@@ -401,7 +401,7 @@
         return pltpu.make_async_copy(source, far.at[side], load_sem.at[1, side])
 
     def start_loads(turn):
-        for side in range(2):
+        def load(side):
             slot, _ = slot_of(turn, side)
             first, second, reach = first_of(slot), second_of(slot), reach_of(slot)
             relative = lax.div(first, orb_dev) ^ member
@@ -437,12 +437,18 @@
                 def _():
                     far_copy(side, one_ref.at[jnp.maximum(own - 1, 0)]).start()
 
+        load(0)
+        pl.when(2 * turn + 1 < found)(functools.partial(load, 1))
+
     def wait_loads(turn):
-        for side in range(2):
+        def wait(side):
             pltpu.make_async_copy(
                 phi_refs[0].at[0], near.at[lax.rem(turn, 2), side], load_sem.at[0, side]
             ).wait()
             far_copy(side, phi_refs[0].at[0]).wait()
+
+        wait(0)
+        pl.when(2 * turn + 1 < found)(functools.partial(wait, 1))
 
     @pl.when(found > 0)
     def _():
@@ -459,11 +465,10 @@
         act_copies = []
         for k in range(groups):
             source = (member ^ k) * slab
-            place = reversed_bits(k, groups)
             act_copies.append(
                 pltpu.make_async_copy(
                     act.at[:, pl.ds(pl.multiple_of(source, ROWS), slab), :],
-                    act_outs[2 * place // groups].at[place % (groups // 2)],
+                    act_outs[k],
                     out_sem.at[3 + k],
                 )
             )
@@ -491,7 +496,7 @@
     def columns(k):
         return pl.ds(pl.multiple_of(k * LANES, LANES), LANES)
 
-    def set_masks(place, delta, weight):
+    def set_masks(place, delta):
         shape = masks.shape[1:]
         spot = lax.broadcasted_iota(jnp.int32, shape, 0) * LANES
         spot = spot + lax.broadcasted_iota(jnp.int32, shape, 1)
@@ -499,7 +504,7 @@
         z = spot - y * edge - delta[2]
         y = y - delta[1]
         inside = (y >= 0) & (y < edge) & (z >= 0) & (z < edge)
-        masks[place] = jnp.where(inside, weight, 0.0)
+        masks[place] = jnp.where(inside, 1.0, 0.0)
 
     def shifted(source, place, delta, begin, count, ks):
         shift = lax.rem(delta[1] * edge + delta[2] + 4 * plane, plane)
@@ -542,20 +547,23 @@
         offsets = [offset_of(slot) for slot, _ in picked]
         returns = [[-d for d in delta] for delta in offsets]
         for side in range(2):
-            set_masks(side, offsets[side], picked[side][1].astype(jnp.float32))
-            set_masks(2 + side, returns[side], 1.0)
-
-        def widen(k):
-            for side in range(2):
+            set_masks(side, offsets[side])
+            set_masks(2 + side, returns[side])
+
+        def with_sides(work):
+            both = 2 * turn + 1 < found
+            pl.when(both)(functools.partial(work, 2))
+            pl.when(jnp.logical_not(both))(functools.partial(work, 1))
+
+        def widen(sides, k):
+            for side in range(sides):
                 wide[side, k, middle, :] = far[side, :, pl.ds(pl.multiple_of(k * LANES, LANES), LANES)]
 
-        steps(chunks, widen, chunks)
-
-        def over_y(t):
+        def over_y(sides_now, t):
             densities = []
             begin = pl.multiple_of(t * ROWS, ROWS)
             rows = pl.ds(begin, ROWS)
-            for side in range(2):
+            for side in range(sides_now):
                 values = shifted(wide.at[side], side, offsets[side], begin, ROWS, range(chunks))
                 for k in range(chunks):
                     moved[side, k, rows, :] = values[k]
@@ -565,7 +573,7 @@
             for y in range(edge):
                 first, offset = divmod(y * edge, LANES)
                 sides = []
-                for side in range(2):
+                for side in range(sides_now):
                     shift = (side * HALF - offset) % LANES
                     value = densities[side][first]
                     value = pltpu.roll(value, shift, 1) if shift else value
@@ -574,7 +582,7 @@
                         more = pltpu.roll(more, shift, 1) if shift else more
                         value = jnp.where(lane < side * HALF + LANES - offset, value, more)
                     sides.append(value)
-                planes.append(Number(jnp.where(lane < HALF, sides[0], sides[1])))
+                planes.append(Number(jnp.where(lane < HALF, sides[0], sides[1] if sides[1:] else 0.0)))
             values = real_dft(planes)
             for i in range(half):
                 at = tile(t, i, edge)
@@ -582,7 +590,11 @@
                 imag = values[i].imag
                 lower[1, at, :] = jnp.zeros((ROWS, LANES), jnp.float32) if imag is None else imag
 
-        steps(tiles, over_y, 3)
+        def densities_over_y(sides):
+            steps(chunks, functools.partial(widen, sides), chunks)
+            steps(tiles, functools.partial(over_y, sides), 3)
+
+        with_sides(densities_over_y)
 
         @pl.when(turn == 0)
         def _():
@@ -617,14 +629,14 @@
 
         firsts = [first_of(slot) for slot, _ in picked]
 
-        def back_y(t):
+        def back_y(sides, t):
             begin = pl.multiple_of(t * ROWS, ROWS)
             rows = pl.ds(begin, ROWS)
             at = [across(t, i, height) for i in range(half)]
             values = [Number(upper[0, a, :], upper[1, a, :]) for a in at]
             values = values + [values[edge - i].conj() for i in range(half, edge)]
             planes = real_back(values)
-            for side in range(2):
+            for side in range(sides):
                 forward = []
                 for k in range(chunks):
                     value = None
@@ -643,7 +655,7 @@
                 for k in range(chunks):
                     act[firsts[side], at[k], :] = sums[k]
 
-        steps(tiles, back_y, 3)
+        with_sides(lambda sides: steps(tiles, functools.partial(back_y, sides), 3))
 
         if second_part:
             @pl.when(turn + 1 == turns)
@@ -656,8 +668,8 @@
             slot = picked[side][0]
             homes.append(reach_of(slot) * orb_dev + lax.rem(second_of(slot), orb_dev))
 
-        def send_back(g):
-            for side in range(2):
+        def send_back(sides, g):
+            for side in range(sides):
                 ks = [g * stretch + i for i in range(stretch)]
                 values = shifted(dense.at[side], 2 + side, returns[side], 0, edge, ks)
                 at = [
@@ -671,7 +683,7 @@
                 for (i, t, a), value in zip(at, sums):
                     back[homes[side], a, :] = value
 
-        steps(chunks // stretch, send_back, 3)
+        with_sides(lambda sides: steps(chunks // stretch, functools.partial(send_back, sides), 3))
         return 0
 
     if second_part:
@@ -701,11 +713,6 @@
         copy.wait()
 
 
-def reversed_bits(k, count):
-    bits = count.bit_length() - 1
-    return sum(((k >> i) & 1) << (bits - 1 - i) for i in range(bits))
-
-
 def pair_terms(numbers, fragments, slots, tables, pieces, far, before=()):
     second_part = bool(before)
     orb_dev, edge, plane = pieces[0].shape
@@ -724,9 +731,9 @@
         return [jax.ShapeDtypeStruct((count, rows, LANES), f32) for count in counts]
 
     if second_part:
-        out_shape = [jax.ShapeDtypeStruct((groups // 2, frag_size, rows // groups, LANES), f32)] * 2
+        out_shape = [jax.ShapeDtypeStruct((frag_size, rows // groups, LANES), f32)] * groups
         out_shape += fields(1, orb_dev - 1, orb_dev)
-        out_specs = [hbm] * 5
+        out_specs = [hbm] * (groups + 3)
         scratch = [pltpu.VMEM(field.shape, f32) for field in fields(frag_size, REACH * orb_dev)]
         scratch += [pltpu.SemaphoreType.DMA((2,)), pltpu.SemaphoreType.DMA((3 + groups,))]
     else:
@@ -827,16 +834,16 @@
     return next(n for n in (72, 24, 8) if length % n == 0)
 
 
-def action_kernel(shape, places_ref, phi_ref, kept_ref, *refs):
-    orb_dev, groups, parts = shape
-    arrived, (act_ref, share_ref) = refs[:parts], refs[parts:]
+def action_kernel(shape, places_ref, phi_ref, *refs):
+    orb_dev, groups = shape
+    parts, (act_ref, share_ref) = refs[:-2], refs[-2:]
     member = places_ref[1]
     frag_size = orb_dev * groups
     slab = act_ref.shape[1]
-    cut = frag_size // parts
-    for i in range(parts):
-        span = slice(i * cut, (i + 1) * cut)
-        act_ref[span] = kept_ref[0, span] + arrived[i][0]
+    value = parts[0][...]
+    for part in parts[1:]:
+        value = value + part[...]
+    act_ref[...] = value
     rows = [(member ^ (a // orb_dev)) * orb_dev + a % orb_dev for a in range(frag_size)]
     result = jnp.zeros(share_ref.shape, jnp.float32)
     for half in range(0, frag_size, 4):
@@ -846,21 +853,21 @@
     share_ref[...] = result
 
 
-def action_terms(places, orb_dev, phi, kept, arrived):
+def action_terms(places, orb_dev, phi, parts):
     frag_size, slab = phi.shape[:2]
     smem = pl.BlockSpec(memory_space=pltpu.SMEM)
     vmem = pl.BlockSpec(memory_space=pltpu.VMEM)
     return pl.pallas_call(
-        functools.partial(action_kernel, (orb_dev, frag_size // orb_dev, len(arrived))),
+        functools.partial(action_kernel, (orb_dev, frag_size // orb_dev)),
         out_shape=(
             jax.ShapeDtypeStruct((frag_size, slab, LANES), jnp.float32),
             jax.ShapeDtypeStruct((frag_size, LANES), jnp.float32),
         ),
-        in_specs=[smem] + [vmem] * (2 + len(arrived)),
+        in_specs=[smem] + [vmem] * (1 + len(parts)),
         out_specs=(vmem, vmem),
         compiler_params=pltpu.CompilerParams(vmem_limit_bytes=16 << 20),
         name="action_terms",
-    )(places, phi, kept, *arrived)
+    )(places, phi, *parts)
 
 
 def home_kernel(shape, places_ref, flat_ref, own_ref, *refs):
@@ -1040,29 +1047,31 @@
     act, two_tail, two_head, back = pair_terms(numbers, *sizes, tables, pieces, [twin, two])
     two_tail, relay, one = together(two_tail, relay, one)
     two_tail = to_fragment(two_tail, 2)
-    kept, sent, one_head, one_tail, own = pair_terms(
+    *acts, one_head, one_tail, own = pair_terms(
         numbers, *sizes, tables, pieces, [twin, relay, one], [act, back]
     )
 
-    sent, two_tail, two_head = together(sent, two_tail, two_head)
+    acts[-1], two_tail, two_head = together(acts[-1], two_tail, two_head)
     two_head = to_fragment(two_head, 2)
     twin = with_twin(one_head)
     bit = 1
-    arrived = with_member(sent, bit)
-    while 2 * bit < groups:
-        kept = kept + arrived
-        if bit == 1:
-            _, twin, one_tail, two_head = together(kept, twin, one_tail, two_head)
-        half = kept.shape[0] // 2
+    parts = {k: [act] for k, act in enumerate(acts)}
+    while bit < groups:
+        for k in sorted(parts, reverse=True):
+            if k & bit:
+                going = sum(parts[k][1:], parts[k][0])
+                if bit == 2:
+                    _, twin, one_tail, two_head = together(going, twin, one_tail, two_head)
+                del parts[k]
+                parts[k ^ bit].append(with_member(going, bit))
         bit *= 2
-        arrived, kept = with_member(kept[half:], bit), kept[:half]
     one_tail = to_fragment(one_tail, 1)
     relay = to_fragment(twin, 2, 0)
 
     flat, phi = flatten_terms(places, pieces)
     tails = home_terms(places, edge, groups, flat, own, 1, two_tail, one_tail)
     tails = by_member(tails)
-    act, share = action_terms(places, orb_dev, phi, kept, [arrived])
+    act, share = action_terms(places, orb_dev, phi, parts[0])
     heads = by_member(
         home_terms(places, edge, groups, flat, own, 0, two_head, twin, relay, share)
     )

time: 107 us -> 107 us (level)
  waiting for transfers between devices: 51 us -> 39.9 us
  Pallas kernels: 24.7 us -> 32.8 us
  local copies, waits for them, and re-layouts: 4.06 us -> 6.66 us
  starting transfers between devices: 24.8 us -> 25.9 us
    ppermute x7, waiting for transfers between devices: 28.5 us -> 19.1 us  [to_fragment(): lax.ppermute(block, 'orb', [(i, (i + distance) % devices) for i in senders])]
    pallas_call x2, Pallas kernels: 13.2 us -> 21.3 us  [pair_terms(): pl.pallas_call(functools.partial(pair_kernel, shape, second_part), out_sh...]
    ppermute x2, starting transfers between devices: 3.81 us -> 6.87 us  [with_twin(): lax.ppermute(block, 'orb', [(i, i ^ 1) for i in range(lax.axis_size('orb'...]
    unnamed x13 -> x9, local copies, waits for them, and re-layouts: 1.01 us -> 3.84 us
    ppermute x13 -> x14, waiting for transfers between devices: 10.9 us -> 8.3 us  [with_member(): lax.ppermute(block, 'grp', [(i, i ^ bit) for i in range(lax.axis_size('gr...]
    ppermute x13 -> x14, starting transfers between devices: 7.81 us -> 6.27 us  [with_member(): lax.ppermute(block, 'grp', [(i, i ^ bit) for i in range(lax.axis_size('gr...]
  transfers between devices with their start and end apart: 22 -> 23, of which waited for: 12 -> 10; matrix products, arithmetic and copies ran while one was open for 3% -> 3% of each run, Pallas kernels for 21% -> 28%
where the time goes in v2:
time: 107 us
  waiting for transfers between devices  39.9 us (37%)
  Pallas kernels  32.8 us (31%)
  starting transfers between devices  25.9 us (24%)
  local copies, waits for them, and re-layouts  6.66 us (6%)
  between operations  1.45 us (1%)
    pallas_call x2, Pallas kernels, pair_terms(): pl.pallas_call(functools.partial(pair_kernel, shape, second_part), out_sh...  21.3 us
    ppermute x7, waiting for transfers between devices, to_fragment(): lax.ppermute(block, 'orb', [(i, (i + distance) % devices) for i in senders])  19.1 us
    ppermute x7, starting transfers between devices, to_fragment(): lax.ppermute(block, 'orb', [(i, (i + distance) % devices) for i in senders])  12.8 us
    ppermute x2, waiting for transfers between devices, with_twin(): lax.ppermute(block, 'orb', [(i, i ^ 1) for i in range(lax.axis_size('orb'...  12.6 us
    ppermute x14, waiting for transfers between devices, with_member(): lax.ppermute(block, 'grp', [(i, i ^ bit) for i in range(lax.axis_size('gr...  8.3 us
    ppermute x2, starting transfers between devices, with_twin(): lax.ppermute(block, 'orb', [(i, i ^ 1) for i in range(lax.axis_size('orb'...  6.87 us
    ppermute x14, starting transfers between devices, with_member(): lax.ppermute(block, 'grp', [(i, i ^ bit) for i in range(lax.axis_size('gr...  6.27 us
    unnamed x9, local copies, waits for them, and re-layouts  3.84 us
  transfers between devices with their start and end apart: 23, of which 10 were waited for; matrix products, arithmetic and copies ran while one was open for 3% of the time, Pallas kernels for 28%

profile of v2, /device:TPU:0, one launch (start us, length us, event | category | flops | bytes accessed | tf_op | source)
XLA Modules:
  0.0 106.9 jit_solution(14569933168879621532)
XLA Ops:
  0.6 5.1 %collective-permute-start.1 = (f32[2,48,2304]{2,1,0:T(8,128)}, f32[2,48,2304]{2,1,0:T(8,128)S(1)}, u32[]{:S(2)}, u32[]{:S(2)}) collective-permute-start(f32[2,48,2304]{2,1,0:T(8,128)} %refs_3_.3), channel_id=1, source_target_pairs={{0,24},{4,28},{8,0},{12,4},{16,8},{20,12},{24,16},{28,20},{1,25},{... | collective-permute-start | bytes 2654216 | tf_op jit(solution)/shard_map/ppermute | solution.py:1000
  5.7 1.5 %collective-permute-start.3 = (f32[2,48,2304]{2,1,0:T(8,128)}, f32[2,48,2304]{2,1,0:T(8,128)S(1)}, u32[]{:S(2)}, u32[]{:S(2)}) collective-permute-start(f32[2,48,2304]{2,1,0:T(8,128)} %refs_3_.3), channel_id=1, source_target_pairs={{0,2},{1,3},{2,0},{3,1},{4,6},{5,7},{6,4},{7,5},{8,10},{9,11},{10,... | collective-permute-start | bytes 2654216 | tf_op jit(solution)/shard_map/ppermute | solution.py:1008
  7.3 2.0 %fusion = (f32[1,48,2304]{2,1,0:T(8,128)S(1)}, f32[1,48,2304]{2,1,0:T(8,128)}) fusion(f32[2,48,2304]{2,1,0:T(8,128)} %refs_3_.3), kind=kLoop, calls=%fused_computation.1 | loop fusion | bytes 1769472 | tf_op jit(solution)/shard_map/slice | solution.py:1039
  9.2 1.5 %collective-permute-start.2 = (f32[1,48,2304]{2,1,0:T(8,128)}, f32[1,48,2304]{2,1,0:T(8,128)S(1)}, u32[]{:S(2)}, u32[]{:S(2)}) collective-permute-start(f32[1,48,2304]{2,1,0:T(8,128)} %get-tuple-element.95), channel_id=1, source_target_pairs={{0,4},{4,0},{8,12},{12,8},{16,20},{20,16},{24,28},{28,24},{1,5},{5... | collective-permute-start | bytes 1327112 | tf_op jit(solution)/shard_map/ppermute | solution.py:1004
  10.7 0.8 copy.11
  12.2 0.8 concatenate.4.numbers_ref
  13.0 1.0 copy-done.2
  14.0 0.9 copy-done.3
  14.9 3.5 %screen_terms.1 = (f32[1536,128]{1,0:T(8,128)S(1)}, s32[51]{0:T(128)S(1)}, bf16[768,256]{1,0:T(8,128)(2,1)S(1)}, bf16[768,256]{1,0:T(8,128)(2,1)S(1)}) custom-call(s32[51]{0:T(128)S(1)} %concatenate.4.numbers_ref, f32[48,2304]{1,0:T(8,128)S(1)} %copy-done.2, bf16[2,2,128,128]{3,2,1,0:T(8,128)(2,1)S(1)} %copy-done.3), custom_call_target="tpu_custom_call" | custom-call | tf_op jit(solution)/shard_map/screen_terms/pallas_call | solution.py:304
  18.4 2.3 %collective-permute-done.2.refs_7_ = f32[1,48,2304]{2,1,0:T(8,128)S(1)} collective-permute-done((f32[1,48,2304]{2,1,0:T(8,128)}, f32[1,48,2304]{2,1,0:T(8,128)S(1)}, u32[]{:S(2)}, u32[]{:S(2)}) %collective-permute-start.2) | collective-permute-done | bytes 442400 | tf_op jit(solution)/shard_map/ppermute | solution.py:1004
  20.8 4.2 %collective-permute-done.1.refs_8_ = f32[2,48,2304]{2,1,0:T(8,128)S(1)} collective-permute-done((f32[2,48,2304]{2,1,0:T(8,128)}, f32[2,48,2304]{2,1,0:T(8,128)S(1)}, u32[]{:S(2)}, u32[]{:S(2)}) %collective-permute-start.1) | collective-permute-done | bytes 884768 | tf_op jit(solution)/shard_map/ppermute | solution.py:1000
  25.0 2.1 %collective-permute-done.3.refs_2_.refs_5_ = f32[2,48,2304]{2,1,0:T(8,128)S(1)} collective-permute-done((f32[2,48,2304]{2,1,0:T(8,128)}, f32[2,48,2304]{2,1,0:T(8,128)S(1)}, u32[]{:S(2)}, u32[]{:S(2)}) %collective-permute-start.3) | collective-permute-done | bytes 884768 | tf_op jit(solution)/shard_map/ppermute | solution.py:1008
  27.7 4.3 %collective-permute-start.6 = (f32[1,48,2304]{2,1,0:T(8,128)S(1)}, f32[1,48,2304]{2,1,0:T(8,128)S(1)}, u32[]{:S(2)}, u32[]{:S(2)}) collective-permute-start(f32[1,48,2304]{2,1,0:T(8,128)S(1)} %get-tuple-element.61), channel_id=1, source_target_pairs={{0,28},{4,0},{8,4},{12,8},{16,12},{20,16},{24,20},{28,24},{1,29},{... | collective-permute-start | bytes 1327112 | tf_op jit(solution)/shard_map/ppermute | solution.py:1000
  32.0 1.2 %copy-done = f32[2,48,2304]{2,1,0:T(8,128)S(1)} copy-done((f32[2,48,2304]{2,1,0:T(8,128)S(1)}, f32[2,48,2304]{2,1,0:T(8,128)}, u32[]{:S(2)}) %copy-start) | copy-done | bytes 884760
  33.2 10.2 %early_pair_terms.1 = (f32[8,864,128]{2,1,0:T(8,128)S(1)}, f32[1,864,128]{2,1,0:T(8,128)S(1)}, f32[1,864,128]{2,1,0:T(8,128)S(1)}, f32[4,864,128]{2,1,0:T(8,128)S(1)}) custom-call(s32[51]{0:T(128)S(1)} %get-tuple-element.54.numbers_ref, f32[1536,128]{1,0:T(8,128)S(1)} %get-tuple-element.55.refs_0_, bf16[768,256]{1,0:T(8,128)(2,1)S(1)} %get-tuple-element.56.refs_1_, ...), custom_call_target="tpu_custom_call" | custom-call | tf_op jit(solution)/shard_map/early_pair_terms/pallas_call | solution.py:744
  43.9 11.1 %late_pair_terms.1 = (f32[8,216,128]{2,1,0:T(8,128)S(1)}, f32[8,216,128]{2,1,0:T(8,128)S(1)}, f32[8,216,128]{2,1,0:T(8,128)S(1)}, f32[8,216,128]{2,1,0:T(8,128)S...) custom-call(s32[51]{0:T(128)S(1)} %get-tuple-element.54.numbers_ref, ...), custom_call_target="tpu_custom_call" | custom-call | tf_op jit(solution)/shard_map/late_pair_terms/pallas_call | solution.py:744
  54.9 1.8 %collective-permute-done.8.refs_0_ = f32[1,864,128]{2,1,0:T(8,128)S(1)} collective-permute-done((f32[1,864,128]{2,1,0:T(8,128)S(1)}, f32[1,864,128]{2,1,0:T(8,128)S(1)}, u32[]{:S(2)}, u32[]{:S(2)}) %collective-permute-start.8) | collective-permute-done | bytes 442400 | tf_op jit(solution)/shard_map/ppermute | solution.py:1000
  56.7 5.4 %collective-permute-start.11 = (f32[1,864,128]{2,1,0:T(8,128)S(1)}, f32[1,864,128]{2,1,0:T(8,128)S(1)}, u32[]{:S(2)}, u32[]{:S(2)}) collective-permute-start(f32[1,864,128]{2,1,0:T(8,128)S(1)} %get-tuple-element.76), channel_id=1, source_target_pairs={{0,4},{4,0},{8,12},{12,8},{16,20},{20,16},{24,28},{28,24},{1,5},{5... | collective-permute-start | bytes 1327112 | tf_op jit(solution)/shard_map/ppermute | solution.py:1004
  62.3 10.2 %collective-permute-done.11.refs_1_ = f32[1,864,128]{2,1,0:T(8,128)S(1)} collective-permute-done((f32[1,864,128]{2,1,0:T(8,128)S(1)}, f32[1,864,128]{2,1,0:T(8,128)S(1)}, u32[]{:S(2)}, u32[]{:S(2)}) %collective-permute-start.11) | collective-permute-done | bytes 442400 | tf_op jit(solution)/shard_map/ppermute | solution.py:1004
  72.5 3.3 %collective-permute-done.12.refs_0_ = f32[1,864,128]{2,1,0:T(8,128)S(1)} collective-permute-done((f32[1,864,128]{2,1,0:T(8,128)S(1)}, f32[1,864,128]{2,1,0:T(8,128)S(1)}, u32[]{:S(2)}, u32[]{:S(2)}) %collective-permute-start.12) | collective-permute-done | bytes 442400 | tf_op jit(solution)/shard_map/ppermute | solution.py:1000
  76.1 1.9 %collective-permute-start.13 = (f32[1,864,128]{2,1,0:T(8,128)S(1)}, f32[1,864,128]{2,1,0:T(8,128)S(1)}, u32[]{:S(2)}, u32[]{:S(2)}) collective-permute-start(f32[1,864,128]{2,1,0:T(8,128)S(1)} %collective-permute-done.11.refs_1_), channel_id=1, source_target_pairs={{0,8},{8,16},{16,24},{24,0},{1,9},{9,17},{17,25},{25,1},{2,10},{10... | collective-permute-start | bytes 1327112 | tf_op jit(solution)/shard_map/ppermute | solution.py:1000
  78.1 1.5 %flatten_terms.1 = (f32[8,864,128]{2,1,0:T(8,128)S(1)}, f32[8,216,128]{2,1,0:T(8,128)S(1)}) custom-call(s32[2]{0:T(128)S(1)} %pad_add_fusion.places_ref, f32[2,48,2304]{2,1,0:T(8,128)S(1)} %copy-done.1, f32[2,48,2304]{2,1,0:T(8,128)S(1)} %collective-permute-done.refs_1_.refs_4_, f32[2,48,2304]{2,1,0:T(8,128)S(1)} %collective-permute-done.3.refs_2_.refs_5_, ...), custom_call_target="tpu_custom_call" | custom-call | tf_op jit(solution)/shard_map/flatten_terms/pallas_call | solution.py:795
  79.6 9.8 %collective-permute-done.18.refs_1_ = f32[1,864,128]{2,1,0:T(8,128)S(1)} collective-permute-done((f32[1,864,128]{2,1,0:T(8,128)S(1)}, f32[1,864,128]{2,1,0:T(8,128)S(1)}, u32[]{:S(2)}, u32[]{:S(2)}) %collective-permute-start.18) | collective-permute-done | bytes 442400 | tf_op jit(solution)/shard_map/ppermute | solution.py:1000
  89.5 1.1 %home_terms.3 = (f32[224,128]{1,0:T(8,128)S(1)}, f32[224,128]{1,0:T(8,128)S(1)}, f32[224,128]{1,0:T(8,128)S(1)}, f32[224,128]{1,0:T(8,128)S(1)}) custom-call(s32[2]{0:T(128)S(1)} %pad_add_fusion.places_ref, f32[8,864,128]{2,1,0:T(8,128)S(1)} %get-tuple-element.74.flat_ref, f32[2,864,128]{2,1,0:T(8,128)S(1)} %get-tuple-element.75.own_ref, ...), custom_call_target="tpu_custom_call" | custom-call | tf_op jit(solution)/shard_map/home_terms/pallas_call | solution.py:916
  90.7 1.6 %action_terms.1 = (f32[8,216,128]{2,1,0:T(8,128)S(1)}, f32[8,128]{1,0:T(8,128)S(1)}) custom-call(s32[2]{0:T(128)S(1)} %pad_add_fusion.places_ref, f32[8,216,128]{2,1,0:T(8,128)S(1)} %get-tuple-element.53.phi_ref, f32[8,216,128]{2,1,0:T(8,128)S(1)} %get-tuple-element.66.refs_0_, f32[8,216,128]{2,1,0:T(8,128)S(1)} %collective-permute-done.7.refs_1_, ...), custom_call_target="tpu_custom_call" | custom-call | tf_op jit(solution)/shard_map/action_terms/pallas_call | solution.py:860
  92.4 1.1 %home_terms.2 = (f32[224,128]{1,0:T(8,128)S(1)}, f32[224,128]{1,0:T(8,128)S(1)}, f32[224,128]{1,0:T(8,128)S(1)}, f32[224,128]{1,0:T(8,128)S(1)}) custom-call(s32[2]{0:T(128)S(1)} %pad_add_fusion.places_ref, f32[8,864,128]{2,1,0:T(8,128)S(1)} %get-tuple-element.74.flat_ref, f32[2,864,128]{2,1,0:T(8,128)S(1)} %get-tuple-element.75.own_ref, ...), custom_call_target="tpu_custom_call" | custom-call | tf_op jit(solution)/shard_map/home_terms/pallas_call | solution.py:916
  93.5 2.0 %collective-permute-start.16 = (f32[224,128]{1,0:T(8,128)S(1)}, f32[224,128]{1,0:T(8,128)S(1)}, u32[]{:S(2)}, u32[]{:S(2)}) collective-permute-start(f32[224,128]{1,0:T(8,128)S(1)} %get-tuple-element.85), channel_id=1, source_target_pairs={{0,2},{1,3},{2,0},{3,1},{4,6},{5,7},{6,4},{7,5},{8,10},{9,11},{10,... | collective-permute-start | bytes 344072 | tf_op jit(solution)/shard_map/ppermute | solution.py:1008
  96.1 1.9 %collective-permute-start.15 = (f32[224,128]{1,0:T(8,128)S(1)}, f32[224,128]{1,0:T(8,128)S(1)}, u32[]{:S(2)}, u32[]{:S(2)}) collective-permute-start(f32[224,128]{1,0:T(8,128)S(1)} %get-tuple-element.84), channel_id=1, source_target_pairs={{0,2},{1,3},{2,0},{3,1},{4,6},{5,7},{6,4},{7,5},{8,10},{9,11},{10,... | collective-permute-start | bytes 344072 | tf_op jit(solution)/shard_map/ppermute | solution.py:1008
  98.0 1.5 %collective-permute-done.16 = f32[224,128]{1,0:T(8,128)S(1)} collective-permute-done((f32[224,128]{1,0:T(8,128)S(1)}, f32[224,128]{1,0:T(8,128)S(1)}, u32[]{:S(2)}, u32[]{:S(2)}) %collective-permute-start.16) | collective-permute-done | bytes 114720 | tf_op jit(solution)/shard_map/ppermute | solution.py:1008
  99.6 2.5 %collective-permute-done.20.refs_6_ = f32[224,128]{1,0:T(8,128)S(1)} collective-permute-done((f32[224,128]{1,0:T(8,128)S(1)}, f32[224,128]{1,0:T(8,128)S(1)}, u32[]{:S(2)}, u32[]{:S(2)}) %collective-permute-start.20) | collective-permute-done | bytes 114720 | tf_op jit(solution)/shard_map/ppermute | solution.py:1008
  102.0 2.2 %collective-permute-done.15.refs_2_ = f32[224,128]{1,0:T(8,128)S(1)} collective-permute-done((f32[224,128]{1,0:T(8,128)S(1)}, f32[224,128]{1,0:T(8,128)S(1)}, u32[]{:S(2)}, u32[]{:S(2)}) %collective-permute-start.15) | collective-permute-done | bytes 114720 | tf_op jit(solution)/shard_map/ppermute | solution.py:1008
  104.2 2.7 %gradient_terms.1 = (f32[12,8,2304]{2,1,0:T(8,128)}, f32[8,8]{1,0:T(8,128)}) custom-call(s32[2]{0:T(128)S(1)} %pad_add_fusion.places_ref, f32[8,216,128]{2,1,0:T(8,128)S(1)} %get-tuple-element.73.act_ref, f32[8,216,128]{2,1,0:T(8,128)S(1)} %get-tuple-element.53.phi_ref, f32[224,128]{1,0:T(8,128)S(1)} %get-tuple-element.82.refs_0_, ...), custom_call_target="tpu_custom_call" | custom-call | tf_op jit(solution)/shard_map/gradient_terms/pallas_call | solution.py:978
  (36 shorter events, 2.6 us)
Async XLA Ops:
  0.6 24.3 %collective-permute-start.1 = (f32[2,48,2304]{2,1,0:T(8,128)}, f32[2,48,2304]{2,1,0:T(8,128)S(1)}, u32[]{:S(2)}, u32[]{:S(2)}) collective-permute-start(f32[2,48,2304]{2,1,0:T(8,128)} %refs_3_.3), channel_id=1, source_target_pairs={{0,24},{4,28},{8,0},{12,4},{16,8},{20,12},{24,16},{28,20},{1,25},{... | collective-permute-start | bytes 2654216 | tf_op jit(solution)/shard_map/ppermute | solution.py:1000
  5.7 21.3 %collective-permute-start.3 = (f32[2,48,2304]{2,1,0:T(8,128)}, f32[2,48,2304]{2,1,0:T(8,128)S(1)}, u32[]{:S(2)}, u32[]{:S(2)}) collective-permute-start(f32[2,48,2304]{2,1,0:T(8,128)} %refs_3_.3), channel_id=1, source_target_pairs={{0,2},{1,3},{2,0},{3,1},{4,6},{5,7},{6,4},{7,5},{8,10},{9,11},{10,... | collective-permute-start | bytes 2654216 | tf_op jit(solution)/shard_map/ppermute | solution.py:1008
  9.2 11.6 %collective-permute-start.2 = (f32[1,48,2304]{2,1,0:T(8,128)}, f32[1,48,2304]{2,1,0:T(8,128)S(1)}, u32[]{:S(2)}, u32[]{:S(2)}) collective-permute-start(f32[1,48,2304]{2,1,0:T(8,128)} %get-tuple-element.95), channel_id=1, source_target_pairs={{0,4},{4,0},{8,12},{12,8},{16,20},{20,16},{24,28},{28,24},{1,5},{5... | collective-permute-start | bytes 1327112 | tf_op jit(solution)/shard_map/ppermute | solution.py:1004
  10.7 21.3 %collective-permute-start = (f32[2,48,2304]{2,1,0:T(8,128)}, f32[2,48,2304]{2,1,0:T(8,128)S(1)}, u32[]{:S(2)}, u32[]{:S(2)}) collective-permute-start(f32[2,48,2304]{2,1,0:T(8,128)} %refs_3_.3), channel_id=1, source_target_pairs={{0,1},{1,0},{2,3},{3,2},{4,5},{5,4},{6,7},{7,6},{8,9},{9,8},{10,11... | collective-permute-start | bytes 2654216 | tf_op jit(solution)/shard_map/ppermute | solution.py:1008
  13.0 1.0 copy-start.2
  14.0 0.9 copy-start.3
  27.0 5.0 %collective-permute-start.4 = (f32[2,48,2304]{2,1,0:T(8,128)S(1)}, f32[2,48,2304]{2,1,0:T(8,128)S(1)}, u32[]{:S(2)}, u32[]{:S(2)}) collective-permute-start(f32[2,48,2304]{2,1,0:T(8,128)S(1)} %collective-permute-done.3.refs_2_.refs_5_), channel_id=1, source_target_pairs={{0,1},{1,0},{2,3},{3,2},{4,5},{5,4},{6,7},{7,6},{8,9},{9,8},{10,11... | collective-permute-start | bytes 2654216 | tf_op jit(solution)/shard_map/ppermute | solution.py:1008
  27.1 16.4 %collective-permute-start.5 = (f32[1,48,2304]{2,1,0:T(8,128)S(1)}, f32[1,48,2304]{2,1,0:T(8,128)S(1)}, u32[]{:S(2)}, u32[]{:S(2)}) collective-permute-start(f32[1,48,2304]{2,1,0:T(8,128)S(1)} %collective-permute-done.2.refs_7_), channel_id=1, source_target_pairs={{4,28},{12,4},{20,12},{28,20},{5,29},{13,5},{21,13},{29,21},{6,30}... | collective-permute-start | bytes 1327112 | tf_op jit(solution)/shard_map/ppermute | solution.py:1000
  27.7 15.7 %collective-permute-start.6 = (f32[1,48,2304]{2,1,0:T(8,128)S(1)}, f32[1,48,2304]{2,1,0:T(8,128)S(1)}, u32[]{:S(2)}, u32[]{:S(2)}) collective-permute-start(f32[1,48,2304]{2,1,0:T(8,128)S(1)} %get-tuple-element.61), channel_id=1, source_target_pairs={{0,28},{4,0},{8,4},{12,8},{16,12},{20,16},{24,20},{28,24},{1,29},{... | collective-permute-start | bytes 1327112 | tf_op jit(solution)/shard_map/ppermute | solution.py:1000
  32.0 1.2 %copy-start = (f32[2,48,2304]{2,1,0:T(8,128)S(1)}, f32[2,48,2304]{2,1,0:T(8,128)}, u32[]{:S(2)}) copy-start(f32[2,48,2304]{2,1,0:T(8,128)} %refs_3_.3) | copy-start | bytes 2654212
  43.4 13.3 %collective-permute-start.8 = (f32[1,864,128]{2,1,0:T(8,128)S(1)}, f32[1,864,128]{2,1,0:T(8,128)S(1)}, u32[]{:S(2)}, u32[]{:S(2)}) collective-permute-start(f32[1,864,128]{2,1,0:T(8,128)S(1)} %get-tuple-element.70), channel_id=1, source_target_pairs={{0,8},{4,12},{8,16},{12,20},{16,24},{20,28},{24,0},{28,4},{1,9},{5... | collective-permute-start | bytes 1327112 | tf_op jit(solution)/shard_map/ppermute | solution.py:1000
  43.9 34.3 %copy-start.1 = (f32[2,48,2304]{2,1,0:T(8,128)S(1)}, f32[2,48,2304]{2,1,0:T(8,128)}, u32[]{:S(2)}) copy-start(f32[2,48,2304]{2,1,0:T(8,128)} %refs_3_.3) | copy-start | bytes 2654212
  56.7 5.4 %collective-permute-start.9 = (f32[8,216,128]{2,1,0:T(8,128)S(1)}, f32[8,216,128]{2,1,0:T(8,128)S(1)}, u32[]{:S(2)}, u32[]{:S(2)}) collective-permute-start(f32[8,216,128]{2,1,0:T(8,128)S(1)} %get-tuple-element.72), channel_id=1, source_target_pairs={{0,1},{1,0},{2,3},{3,2},{4,5},{5,4},{6,7},{7,6},{8,9},{9,8},{10,11... | collective-permute-start | bytes 2654216 | tf_op jit(solution)/shard_map/ppermute | solution.py:1008
  56.7 15.8 %collective-permute-start.11 = (f32[1,864,128]{2,1,0:T(8,128)S(1)}, f32[1,864,128]{2,1,0:T(8,128)S(1)}, u32[]{:S(2)}, u32[]{:S(2)}) collective-permute-start(f32[1,864,128]{2,1,0:T(8,128)S(1)} %get-tuple-element.76), channel_id=1, source_target_pairs={{0,4},{4,0},{8,12},{12,8},{16,20},{20,16},{24,28},{28,24},{1,5},{5... | collective-permute-start | bytes 1327112 | tf_op jit(solution)/shard_map/ppermute | solution.py:1004
  62.1 13.7 %collective-permute-start.12 = (f32[1,864,128]{2,1,0:T(8,128)S(1)}, f32[1,864,128]{2,1,0:T(8,128)S(1)}, u32[]{:S(2)}, u32[]{:S(2)}) collective-permute-start(f32[1,864,128]{2,1,0:T(8,128)S(1)} %get-tuple-element.78), channel_id=1, source_target_pairs={{0,8},{4,12},{8,16},{12,20},{16,24},{20,28},{24,0},{28,4},{1,9},{5... | collective-permute-start | bytes 1327112 | tf_op jit(solution)/shard_map/ppermute | solution.py:1000
  62.1 28.6 %collective-permute-start.7 = (f32[8,216,128]{2,1,0:T(8,128)S(1)}, f32[8,216,128]{2,1,0:T(8,128)S(1)}, u32[]{:S(2)}, u32[]{:S(2)}) collective-permute-start(f32[8,216,128]{2,1,0:T(8,128)S(1)} %get-tuple-element.67), channel_id=1, source_target_pairs={{0,1},{1,0},{2,3},{3,2},{4,5},{5,4},{6,7},{7,6},{8,9},{9,8},{10,11... | collective-permute-start | bytes 2654216 | tf_op jit(solution)/shard_map/ppermute | solution.py:1008
  62.2 28.5 %collective-permute-start.10 = (f32[8,216,128]{2,1,0:T(8,128)S(1)}, f32[8,216,128]{2,1,0:T(8,128)S(1)}, u32[]{:S(2)}, u32[]{:S(2)}) collective-permute-start(f32[8,216,128]{2,1,0:T(8,128)S(1)} %add.3), channel_id=1, source_target_pairs={{0,2},{1,3},{2,0},{3,1},{4,6},{5,7},{6,4},{7,5},{8,10},{9,11},{10,... | collective-permute-start | bytes 2654216 | tf_op jit(solution)/shard_map/ppermute | solution.py:1008
  75.8 13.7 %collective-permute-start.18 = (f32[1,864,128]{2,1,0:T(8,128)S(1)}, f32[1,864,128]{2,1,0:T(8,128)S(1)}, u32[]{:S(2)}, u32[]{:S(2)}) collective-permute-start(f32[1,864,128]{2,1,0:T(8,128)S(1)} %get-tuple-element.87), channel_id=1, source_target_pairs={{0,4},{4,8},{8,12},{12,16},{16,20},{20,24},{24,28},{28,0},{1,5},{5... | collective-permute-start | bytes 1327112 | tf_op jit(solution)/shard_map/ppermute | solution.py:1000
  76.1 16.2 %collective-permute-start.13 = (f32[1,864,128]{2,1,0:T(8,128)S(1)}, f32[1,864,128]{2,1,0:T(8,128)S(1)}, u32[]{:S(2)}, u32[]{:S(2)}) collective-permute-start(f32[1,864,128]{2,1,0:T(8,128)S(1)} %collective-permute-done.11.refs_1_), channel_id=1, source_target_pairs={{0,8},{8,16},{16,24},{24,0},{1,9},{9,17},{17,25},{25,1},{2,10},{10... | collective-permute-start | bytes 1327112 | tf_op jit(solution)/shard_map/ppermute | solution.py:1000
  90.6 5.0 %collective-permute-start.21 = (f32[224,128]{1,0:T(8,128)S(1)}, f32[224,128]{1,0:T(8,128)S(1)}, u32[]{:S(2)}, u32[]{:S(2)}) collective-permute-start(f32[224,128]{1,0:T(8,128)S(1)} %get-tuple-element.91), channel_id=1, source_target_pairs={{0,2},{1,3},{2,0},{3,1},{4,6},{5,7},{6,4},{7,5},{8,10},{9,11},{10,... | collective-permute-start | bytes 344072 | tf_op jit(solution)/shard_map/ppermute | solution.py:1008
  90.6 5.4 %collective-permute-start.19 = (f32[224,128]{1,0:T(8,128)S(1)}, f32[224,128]{1,0:T(8,128)S(1)}, u32[]{:S(2)}, u32[]{:S(2)}) collective-permute-start(f32[224,128]{1,0:T(8,128)S(1)} %get-tuple-element.89), channel_id=1, source_target_pairs={{0,1},{1,0},{2,3},{3,2},{4,5},{5,4},{6,7},{7,6},{8,9},{9,8},{10,11... | collective-permute-start | bytes 344072 | tf_op jit(solution)/shard_map/ppermute | solution.py:1008
  93.5 6.1 %collective-permute-start.16 = (f32[224,128]{1,0:T(8,128)S(1)}, f32[224,128]{1,0:T(8,128)S(1)}, u32[]{:S(2)}, u32[]{:S(2)}) collective-permute-start(f32[224,128]{1,0:T(8,128)S(1)} %get-tuple-element.85), channel_id=1, source_target_pairs={{0,2},{1,3},{2,0},{3,1},{4,6},{5,7},{6,4},{7,5},{8,10},{9,11},{10,... | collective-permute-start | bytes 344072 | tf_op jit(solution)/shard_map/ppermute | solution.py:1008
  95.5 6.6 %collective-permute-start.20 = (f32[224,128]{1,0:T(8,128)S(1)}, f32[224,128]{1,0:T(8,128)S(1)}, u32[]{:S(2)}, u32[]{:S(2)}) collective-permute-start(f32[224,128]{1,0:T(8,128)S(1)} %get-tuple-element.90), channel_id=1, source_target_pairs={{0,2},{1,3},{2,0},{3,1},{4,6},{5,7},{6,4},{7,5},{8,10},{9,11},{10,... | collective-permute-start | bytes 344072 | tf_op jit(solution)/shard_map/ppermute | solution.py:1008
  95.6 6.4 %collective-permute-start.22 = (f32[224,128]{1,0:T(8,128)S(1)}, f32[224,128]{1,0:T(8,128)S(1)}, u32[]{:S(2)}, u32[]{:S(2)}) collective-permute-start(f32[224,128]{1,0:T(8,128)S(1)} %collective-permute-done.21), channel_id=1, source_target_pairs={{0,1},{1,0},{2,3},{3,2},{4,5},{5,4},{6,7},{7,6},{8,9},{9,8},{10,11... | collective-permute-start | bytes 344072 | tf_op jit(solution)/shard_map/ppermute | solution.py:1008
  95.8 6.3 %collective-permute-start.14 = (f32[224,128]{1,0:T(8,128)S(1)}, f32[224,128]{1,0:T(8,128)S(1)}, u32[]{:S(2)}, u32[]{:S(2)}) collective-permute-start(f32[224,128]{1,0:T(8,128)S(1)} %get-tuple-element.83), channel_id=1, source_target_pairs={{0,1},{1,0},{2,3},{3,2},{4,5},{5,4},{6,7},{7,6},{8,9},{9,8},{10,11... | collective-permute-start | bytes 344072 | tf_op jit(solution)/shard_map/ppermute | solution.py:1008
  96.1 8.1 %collective-permute-start.15 = (f32[224,128]{1,0:T(8,128)S(1)}, f32[224,128]{1,0:T(8,128)S(1)}, u32[]{:S(2)}, u32[]{:S(2)}) collective-permute-start(f32[224,128]{1,0:T(8,128)S(1)} %get-tuple-element.84), channel_id=1, source_target_pairs={{0,2},{1,3},{2,0},{3,1},{4,6},{5,7},{6,4},{7,5},{8,10},{9,11},{10,... | collective-permute-start | bytes 344072 | tf_op jit(solution)/shard_map/ppermute | solution.py:1008
  99.6 4.6 %collective-permute-start.17 = (f32[224,128]{1,0:T(8,128)S(1)}, f32[224,128]{1,0:T(8,128)S(1)}, u32[]{:S(2)}, u32[]{:S(2)}) collective-permute-start(f32[224,128]{1,0:T(8,128)S(1)} %collective-permute-done.16), channel_id=1, source_target_pairs={{0,1},{1,0},{2,3},{3,2},{4,5},{5,4},{6,7},{7,6},{8,9},{9,8},{10,11... | collective-permute-start | bytes 344072 | tf_op jit(solution)/shard_map/ppermute | solution.py:1008

commit v3 on v2

--- a/solution.py
+++ b/solution.py
@@ -873,9 +873,9 @@
 def home_kernel(shape, places_ref, flat_ref, own_ref, *refs):
     edge, orb_dev, groups, first, count = shape
     if first == 0:
-        (two_ref, twin_ref, relay_ref, share_ref), refs = refs[:4], refs[4:]
+        (two_ref, twin_ref, relay_ref), refs = refs[:3], refs[3:]
     else:
-        (two_ref, one_ref), refs = refs[:2], refs[2:]
+        (two_ref, one_ref, share_ref), refs = refs[:3], refs[3:]
     outs, total = refs[:groups], refs[groups]
     fragment, member = places_ref[0], places_ref[1]
     frag_size = orb_dev * groups
@@ -895,7 +895,7 @@
             total[i] = value + one_ref[i]
     lefts, rights = [(flat_ref, a) for a in range(frag_size)], [(total, i) for i in range(count)]
     places = [(member ^ (a // orb_dev)) * orb_dev + a % orb_dev for a in range(frag_size)]
-    result = share_ref[...] if first == 0 else jnp.zeros((frag_size, LANES), jnp.float32)
+    result = jnp.zeros((frag_size, LANES), jnp.float32) if first == 0 else share_ref[...]
     sums = products(lefts, rights, rows, step_of(rows))
     result = placed(result, sums, places, [member * orb_dev + first + i for i in range(count)])
     result = result * (1.0 / float(edge**3))
@@ -1069,12 +1069,11 @@
     relay = to_fragment(twin, 2, 0)
 
     flat, phi = flatten_terms(places, pieces)
-    tails = home_terms(places, edge, groups, flat, own, 1, two_tail, one_tail)
-    tails = by_member(tails)
     act, share = action_terms(places, orb_dev, phi, parts[0])
-    heads = by_member(
-        home_terms(places, edge, groups, flat, own, 0, two_head, twin, relay, share)
-    )
+    share, relay = together(share, relay)
+    tails = home_terms(places, edge, groups, flat, own, 1, two_tail, one_tail, share)
+    heads = home_terms(places, edge, groups, flat, own, 0, two_head, twin, relay)
+    tails, heads = by_member(tails), by_member(heads)
     gradient, lagrange = gradient_terms(places, edge, act, phi, heads, tails)
     return (gradient, lagrange[None])
 

time: 107 us -> 107 us (level)
  waiting for transfers between devices: 39.9 us -> 44.1 us
  Pallas kernels: 32.8 us -> 29.3 us
    ppermute x14, waiting for transfers between devices: 8.3 us -> 13.3 us  [with_member(): lax.ppermute(block, 'grp', [(i, i ^ bit) for i in range(lax.axis_size('gr...]
    pallas_call x2, Pallas kernels: 21.3 us -> 17.8 us  [pair_terms(): pl.pallas_call(functools.partial(pair_kernel, shape, second_part), out_sh...]
    ppermute x2, starting transfers between devices: 6.87 us -> 3.81 us  [with_twin(): lax.ppermute(block, 'orb', [(i, i ^ 1) for i in range(lax.axis_size('orb'...]
    ppermute x14, starting transfers between devices: 6.27 us -> 8.54 us  [with_member(): lax.ppermute(block, 'grp', [(i, i ^ bit) for i in range(lax.axis_size('gr...]
    ppermute x2, waiting for transfers between devices: 12.6 us -> 11.3 us  [with_twin(): lax.ppermute(block, 'orb', [(i, i ^ 1) for i in range(lax.axis_size('orb'...]
  transfers between devices with their start and end apart: 23 -> 23, of which waited for: 10 -> 14; matrix products, arithmetic and copies ran while one was open for 3% -> 4% of each run, Pallas kernels for 28% -> 24%
where the time goes in v3:
time: 107 us
  waiting for transfers between devices  44.1 us (41%)
  Pallas kernels  29.3 us (27%)
  starting transfers between devices  25.1 us (23%)
  local copies, waits for them, and re-layouts  6.66 us (6%)
  between operations  1.41 us (1%)
    ppermute x7, waiting for transfers between devices, to_fragment(): lax.ppermute(block, 'orb', [(i, (i + distance) % devices) for i in senders])  19.5 us
    pallas_call x2, Pallas kernels, pair_terms(): pl.pallas_call(functools.partial(pair_kernel, shape, second_part), out_sh...  17.8 us
    ppermute x14, waiting for transfers between devices, with_member(): lax.ppermute(block, 'grp', [(i, i ^ bit) for i in range(lax.axis_size('gr...  13.3 us
    ppermute x7, starting transfers between devices, to_fragment(): lax.ppermute(block, 'orb', [(i, (i + distance) % devices) for i in senders])  12.8 us
    ppermute x2, waiting for transfers between devices, with_twin(): lax.ppermute(block, 'orb', [(i, i ^ 1) for i in range(lax.axis_size('orb'...  11.3 us
    ppermute x14, starting transfers between devices, with_member(): lax.ppermute(block, 'grp', [(i, i ^ bit) for i in range(lax.axis_size('gr...  8.54 us
    unnamed x9, local copies, waits for them, and re-layouts  3.84 us
    ppermute x2, starting transfers between devices, with_twin(): lax.ppermute(block, 'orb', [(i, i ^ 1) for i in range(lax.axis_size('orb'...  3.81 us
  transfers between devices with their start and end apart: 23, of which 14 were waited for; matrix products, arithmetic and copies ran while one was open for 4% of the time, Pallas kernels for 24%

profile of v3, /device:TPU:0, one launch (start us, length us, event | category | flops | bytes accessed | tf_op | source)
XLA Modules:
  0.0 106.7 jit_solution(7110409425218406676)
XLA Ops:
  0.6 5.1 %collective-permute-start.1 = (f32[2,48,2304]{2,1,0:T(8,128)}, f32[2,48,2304]{2,1,0:T(8,128)S(1)}, u32[]{:S(2)}, u32[]{:S(2)}) collective-permute-start(f32[2,48,2304]{2,1,0:T(8,128)} %refs_3_.3), channel_id=1, source_target_pairs={{0,24},{4,28},{8,0},{12,4},{16,8},{20,12},{24,16},{28,20},{1,25},{... | collective-permute-start | bytes 2654216 | tf_op jit(solution)/shard_map/ppermute | solution.py:1000
  5.7 1.5 %collective-permute-start.3 = (f32[2,48,2304]{2,1,0:T(8,128)}, f32[2,48,2304]{2,1,0:T(8,128)S(1)}, u32[]{:S(2)}, u32[]{:S(2)}) collective-permute-start(f32[2,48,2304]{2,1,0:T(8,128)} %refs_3_.3), channel_id=1, source_target_pairs={{0,2},{1,3},{2,0},{3,1},{4,6},{5,7},{6,4},{7,5},{8,10},{9,11},{10,... | collective-permute-start | bytes 2654216 | tf_op jit(solution)/shard_map/ppermute | solution.py:1008
  7.3 2.0 %fusion = (f32[1,48,2304]{2,1,0:T(8,128)S(1)}, f32[1,48,2304]{2,1,0:T(8,128)}) fusion(f32[2,48,2304]{2,1,0:T(8,128)} %refs_3_.3), kind=kLoop, calls=%fused_computation.1 | loop fusion | bytes 1769472 | tf_op jit(solution)/shard_map/slice | solution.py:1039
  9.2 1.5 %collective-permute-start.2 = (f32[1,48,2304]{2,1,0:T(8,128)}, f32[1,48,2304]{2,1,0:T(8,128)S(1)}, u32[]{:S(2)}, u32[]{:S(2)}) collective-permute-start(f32[1,48,2304]{2,1,0:T(8,128)} %get-tuple-element.99), channel_id=1, source_target_pairs={{0,4},{4,0},{8,12},{12,8},{16,20},{20,16},{24,28},{28,24},{1,5},{5... | collective-permute-start | bytes 1327112 | tf_op jit(solution)/shard_map/ppermute | solution.py:1004
  14.9 3.5 %screen_terms.1 = (f32[1536,128]{1,0:T(8,128)S(1)}, s32[51]{0:T(128)S(1)}, bf16[768,256]{1,0:T(8,128)(2,1)S(1)}, bf16[768,256]{1,0:T(8,128)(2,1)S(1)}) custom-call(s32[51]{0:T(128)S(1)} %concatenate.4.numbers_ref, f32[48,2304]{1,0:T(8,128)S(1)} %copy-done.2, bf16[2,2,128,128]{3,2,1,0:T(8,128)(2,1)S(1)} %copy-done.3), custom_call_target="tpu_custom_call" | custom-call | tf_op jit(solution)/shard_map/screen_terms/pallas_call | solution.py:304
  18.4 2.3 %collective-permute-done.2.refs_7_ = f32[1,48,2304]{2,1,0:T(8,128)S(1)} collective-permute-done((f32[1,48,2304]{2,1,0:T(8,128)}, f32[1,48,2304]{2,1,0:T(8,128)S(1)}, u32[]{:S(2)}, u32[]{:S(2)}) %collective-permute-start.2) | collective-permute-done | bytes 442400 | tf_op jit(solution)/shard_map/ppermute | solution.py:1004
  20.8 4.2 %collective-permute-done.1.refs_8_ = f32[2,48,2304]{2,1,0:T(8,128)S(1)} collective-permute-done((f32[2,48,2304]{2,1,0:T(8,128)}, f32[2,48,2304]{2,1,0:T(8,128)S(1)}, u32[]{:S(2)}, u32[]{:S(2)}) %collective-permute-start.1) | collective-permute-done | bytes 884768 | tf_op jit(solution)/shard_map/ppermute | solution.py:1000
  25.0 2.1 %collective-permute-done.3.refs_2_.refs_5_ = f32[2,48,2304]{2,1,0:T(8,128)S(1)} collective-permute-done((f32[2,48,2304]{2,1,0:T(8,128)}, f32[2,48,2304]{2,1,0:T(8,128)S(1)}, u32[]{:S(2)}, u32[]{:S(2)}) %collective-permute-start.3) | collective-permute-done | bytes 884768 | tf_op jit(solution)/shard_map/ppermute | solution.py:1008
  27.7 4.3 %collective-permute-start.6 = (f32[1,48,2304]{2,1,0:T(8,128)S(1)}, f32[1,48,2304]{2,1,0:T(8,128)S(1)}, u32[]{:S(2)}, u32[]{:S(2)}) collective-permute-start(f32[1,48,2304]{2,1,0:T(8,128)S(1)} %get-tuple-element.63), channel_id=1, source_target_pairs={{0,28},{4,0},{8,4},{12,8},{16,12},{20,16},{24,20},{28,24},{1,29},{... | collective-permute-start | bytes 1327112 | tf_op jit(solution)/shard_map/ppermute | solution.py:1000
  32.0 1.2 %copy-done = f32[2,48,2304]{2,1,0:T(8,128)S(1)} copy-done((f32[2,48,2304]{2,1,0:T(8,128)S(1)}, f32[2,48,2304]{2,1,0:T(8,128)}, u32[]{:S(2)}) %copy-start) | copy-done | bytes 884760
  33.2 8.4 %early_pair_terms.1 = (f32[8,864,128]{2,1,0:T(8,128)S(1)}, f32[1,864,128]{2,1,0:T(8,128)S(1)}, f32[1,864,128]{2,1,0:T(8,128)S(1)}, f32[4,864,128]{2,1,0:T(8,128)S(1)}) custom-call(s32[51]{0:T(128)S(1)} %get-tuple-element.56.numbers_ref, f32[1536,128]{1,0:T(8,128)S(1)} %get-tuple-element.57.refs_0_, bf16[768,256]{1,0:T(8,128)(2,1)S(1)} %get-tuple-element.58.refs_1_, ...), custom_call_target="tpu_custom_call" | custom-call | tf_op jit(solution)/shard_map/early_pair_terms/pallas_call | solution.py:744
  41.7 1.5 %collective-permute-done.6.refs_9_ = f32[1,48,2304]{2,1,0:T(8,128)S(1)} collective-permute-done((f32[1,48,2304]{2,1,0:T(8,128)S(1)}, f32[1,48,2304]{2,1,0:T(8,128)S(1)}, u32[]{:S(2)}, u32[]{:S(2)}) %collective-permute-start.6) | collective-permute-done | bytes 442400 | tf_op jit(solution)/shard_map/ppermute | solution.py:1000
  43.9 9.3 %late_pair_terms.1 = (f32[8,216,128]{2,1,0:T(8,128)S(1)}, f32[8,216,128]{2,1,0:T(8,128)S(1)}, f32[8,216,128]{2,1,0:T(8,128)S(1)}, f32[8,216,128]{2,1,0:T(8,128)S...) custom-call(s32[51]{0:T(128)S(1)} %get-tuple-element.56.numbers_ref, ...), custom_call_target="tpu_custom_call" | custom-call | tf_op jit(solution)/shard_map/late_pair_terms/pallas_call | solution.py:744
  53.2 3.5 %collective-permute-done.8.refs_0_ = f32[1,864,128]{2,1,0:T(8,128)S(1)} collective-permute-done((f32[1,864,128]{2,1,0:T(8,128)S(1)}, f32[1,864,128]{2,1,0:T(8,128)S(1)}, u32[]{:S(2)}, u32[]{:S(2)}) %collective-permute-start.8) | collective-permute-done | bytes 442400 | tf_op jit(solution)/shard_map/ppermute | solution.py:1000
  56.7 2.3 %collective-permute-start.11 = (f32[1,864,128]{2,1,0:T(8,128)S(1)}, f32[1,864,128]{2,1,0:T(8,128)S(1)}, u32[]{:S(2)}, u32[]{:S(2)}) collective-permute-start(f32[1,864,128]{2,1,0:T(8,128)S(1)} %get-tuple-element.78), channel_id=1, source_target_pairs={{0,4},{4,0},{8,12},{12,8},{16,20},{20,16},{24,28},{28,24},{1,5},{5... | collective-permute-start | bytes 1327112 | tf_op jit(solution)/shard_map/ppermute | solution.py:1004
  59.4 1.6 %collective-permute-start.10 = (f32[8,216,128]{2,1,0:T(8,128)S(1)}, f32[8,216,128]{2,1,0:T(8,128)S(1)}, u32[]{:S(2)}, u32[]{:S(2)}) collective-permute-start(f32[8,216,128]{2,1,0:T(8,128)S(1)} %add.3), channel_id=1, source_target_pairs={{0,2},{1,3},{2,0},{3,1},{4,6},{5,7},{6,4},{7,5},{8,10},{9,11},{10,... | collective-permute-start | bytes 2654216 | tf_op jit(solution)/shard_map/ppermute | solution.py:1008
  61.0 8.9 %collective-permute-done.11.refs_1_ = f32[1,864,128]{2,1,0:T(8,128)S(1)} collective-permute-done((f32[1,864,128]{2,1,0:T(8,128)S(1)}, f32[1,864,128]{2,1,0:T(8,128)S(1)}, u32[]{:S(2)}, u32[]{:S(2)}) %collective-permute-start.11) | collective-permute-done | bytes 442400 | tf_op jit(solution)/shard_map/ppermute | solution.py:1004
  69.9 3.5 %collective-permute-done.12.refs_0_ = f32[1,864,128]{2,1,0:T(8,128)S(1)} collective-permute-done((f32[1,864,128]{2,1,0:T(8,128)S(1)}, f32[1,864,128]{2,1,0:T(8,128)S(1)}, u32[]{:S(2)}, u32[]{:S(2)}) %collective-permute-start.12) | collective-permute-done | bytes 442400 | tf_op jit(solution)/shard_map/ppermute | solution.py:1000
  73.4 1.9 %collective-permute-start.13 = (f32[1,864,128]{2,1,0:T(8,128)S(1)}, f32[1,864,128]{2,1,0:T(8,128)S(1)}, u32[]{:S(2)}, u32[]{:S(2)}) collective-permute-start(f32[1,864,128]{2,1,0:T(8,128)S(1)} %collective-permute-done.11.refs_1_), channel_id=1, source_target_pairs={{0,8},{8,16},{16,24},{24,0},{1,9},{9,17},{17,25},{25,1},{2,10},{10... | collective-permute-start | bytes 1327112 | tf_op jit(solution)/shard_map/ppermute | solution.py:1000
  75.5 1.5 %flatten_terms.1 = (f32[8,864,128]{2,1,0:T(8,128)S(1)}, f32[8,216,128]{2,1,0:T(8,128)S(1)}) custom-call(s32[2]{0:T(128)S(1)} %pad_add_fusion.places_ref, f32[2,48,2304]{2,1,0:T(8,128)S(1)} %copy-done.1, f32[2,48,2304]{2,1,0:T(8,128)S(1)} %collective-permute-done.refs_1_.refs_4_, f32[2,48,2304]{2,1,0:T(8,128)S(1)} %collective-permute-done.3.refs_2_.refs_5_, ...), custom_call_target="tpu_custom_call" | custom-call | tf_op jit(solution)/shard_map/flatten_terms/pallas_call | solution.py:795
  77.0 4.3 %collective-permute-done.10.refs_2_ = f32[8,216,128]{2,1,0:T(8,128)S(1)} collective-permute-done((f32[8,216,128]{2,1,0:T(8,128)S(1)}, f32[8,216,128]{2,1,0:T(8,128)S(1)}, u32[]{:S(2)}, u32[]{:S(2)}) %collective-permute-start.10) | collective-permute-done | bytes 884768 | tf_op jit(solution)/shard_map/ppermute | solution.py:1008
  81.3 1.6 %action_terms.1 = (f32[8,216,128]{2,1,0:T(8,128)S(1)}, f32[8,128]{1,0:T(8,128)S(1)}) custom-call(s32[2]{0:T(128)S(1)} %pad_add_fusion.places_ref, f32[8,216,128]{2,1,0:T(8,128)S(1)} %get-tuple-element.55.phi_ref, f32[8,216,128]{2,1,0:T(8,128)S(1)} %get-tuple-element.68.refs_0_, f32[8,216,128]{2,1,0:T(8,128)S(1)} %collective-permute-done.7.refs_1_, ...), custom_call_target="tpu_custom_call" | custom-call | tf_op jit(solution)/shard_map/action_terms/pallas_call | solution.py:860
  82.9 5.8 %collective-permute-done.13.refs_2_ = f32[1,864,128]{2,1,0:T(8,128)S(1)} collective-permute-done((f32[1,864,128]{2,1,0:T(8,128)S(1)}, f32[1,864,128]{2,1,0:T(8,128)S(1)}, u32[]{:S(2)}, u32[]{:S(2)}) %collective-permute-start.13) | collective-permute-done | bytes 442400 | tf_op jit(solution)/shard_map/ppermute | solution.py:1000
  89.7 1.1 %home_terms.3 = (f32[224,128]{1,0:T(8,128)S(1)}, f32[224,128]{1,0:T(8,128)S(1)}, f32[224,128]{1,0:T(8,128)S(1)}, f32[224,128]{1,0:T(8,128)S(1)}) custom-call(s32[2]{0:T(128)S(1)} %pad_add_fusion.places_ref, f32[8,864,128]{2,1,0:T(8,128)S(1)} %get-tuple-element.76.flat_ref, f32[2,864,128]{2,1,0:T(8,128)S(1)} %get-tuple-element.77.own_ref, ...), custom_call_target="tpu_custom_call" | custom-call | tf_op jit(solution)/shard_map/home_terms/pallas_call | solution.py:916
  90.7 1.6 %collective-permute-start.21 = (f32[224,128]{1,0:T(8,128)S(1)}, f32[224,128]{1,0:T(8,128)S(1)}, u32[]{:S(2)}, u32[]{:S(2)}) collective-permute-start(f32[224,128]{1,0:T(8,128)S(1)} %get-tuple-element.95), channel_id=1, source_target_pairs={{0,2},{1,3},{2,0},{3,1},{4,6},{5,7},{6,4},{7,5},{8,10},{9,11},{10,... | collective-permute-start | bytes 344072 | tf_op jit(solution)/shard_map/ppermute | solution.py:1008
  92.3 1.1 %home_terms.2 = (f32[224,128]{1,0:T(8,128)S(1)}, f32[224,128]{1,0:T(8,128)S(1)}, f32[224,128]{1,0:T(8,128)S(1)}, f32[224,128]{1,0:T(8,128)S(1)}) custom-call(s32[2]{0:T(128)S(1)} %pad_add_fusion.places_ref, f32[8,864,128]{2,1,0:T(8,128)S(1)} %get-tuple-element.76.flat_ref, f32[2,864,128]{2,1,0:T(8,128)S(1)} %get-tuple-element.77.own_ref, ...), custom_call_target="tpu_custom_call" | custom-call | tf_op jit(solution)/shard_map/home_terms/pallas_call | solution.py:916
  94.0 1.5 %collective-permute-start.20 = (f32[224,128]{1,0:T(8,128)S(1)}, f32[224,128]{1,0:T(8,128)S(1)}, u32[]{:S(2)}, u32[]{:S(2)}) collective-permute-start(f32[224,128]{1,0:T(8,128)S(1)} %get-tuple-element.94), channel_id=1, source_target_pairs={{0,2},{1,3},{2,0},{3,1},{4,6},{5,7},{6,4},{7,5},{8,10},{9,11},{10,... | collective-permute-start | bytes 344072 | tf_op jit(solution)/shard_map/ppermute | solution.py:1008
  95.6 1.5 %collective-permute-start.15 = (f32[224,128]{1,0:T(8,128)S(1)}, f32[224,128]{1,0:T(8,128)S(1)}, u32[]{:S(2)}, u32[]{:S(2)}) collective-permute-start(f32[224,128]{1,0:T(8,128)S(1)} %get-tuple-element.87), channel_id=1, source_target_pairs={{0,2},{1,3},{2,0},{3,1},{4,6},{5,7},{6,4},{7,5},{8,10},{9,11},{10,... | collective-permute-start | bytes 344072 | tf_op jit(solution)/shard_map/ppermute | solution.py:1008
  97.1 2.3 %collective-permute-done.16 = f32[224,128]{1,0:T(8,128)S(1)} collective-permute-done((f32[224,128]{1,0:T(8,128)S(1)}, f32[224,128]{1,0:T(8,128)S(1)}, u32[]{:S(2)}, u32[]{:S(2)}) %collective-permute-start.16) | collective-permute-done | bytes 114720 | tf_op jit(solution)/shard_map/ppermute | solution.py:1008
  99.4 2.5 %collective-permute-done.20.refs_6_ = f32[224,128]{1,0:T(8,128)S(1)} collective-permute-done((f32[224,128]{1,0:T(8,128)S(1)}, f32[224,128]{1,0:T(8,128)S(1)}, u32[]{:S(2)}, u32[]{:S(2)}) %collective-permute-start.20) | collective-permute-done | bytes 114720 | tf_op jit(solution)/shard_map/ppermute | solution.py:1008
  101.9 2.1 %collective-permute-done.15.refs_2_ = f32[224,128]{1,0:T(8,128)S(1)} collective-permute-done((f32[224,128]{1,0:T(8,128)S(1)}, f32[224,128]{1,0:T(8,128)S(1)}, u32[]{:S(2)}, u32[]{:S(2)}) %collective-permute-start.15) | collective-permute-done | bytes 114720 | tf_op jit(solution)/shard_map/ppermute | solution.py:1008
  104.0 2.7 %gradient_terms.1 = (f32[12,8,2304]{2,1,0:T(8,128)}, f32[8,8]{1,0:T(8,128)}) custom-call(s32[2]{0:T(128)S(1)} %pad_add_fusion.places_ref, f32[8,216,128]{2,1,0:T(8,128)S(1)} %get-tuple-element.75.act_ref, f32[8,216,128]{2,1,0:T(8,128)S(1)} %get-tuple-element.55.phi_ref, f32[224,128]{1,0:T(8,128)S(1)} %get-tuple-element.85.refs_0_, ...), custom_call_target="tpu_custom_call" | custom-call | tf_op jit(solution)/shard_map/gradient_terms/pallas_call | solution.py:978
  (36 shorter events, 7.1 us)
Async XLA Ops:
  0.6 24.3 %collective-permute-start.1 = (f32[2,48,2304]{2,1,0:T(8,128)}, f32[2,48,2304]{2,1,0:T(8,128)S(1)}, u32[]{:S(2)}, u32[]{:S(2)}) collective-permute-start(f32[2,48,2304]{2,1,0:T(8,128)} %refs_3_.3), channel_id=1, source_target_pairs={{0,24},{4,28},{8,0},{12,4},{16,8},{20,12},{24,16},{28,20},{1,25},{... | collective-permute-start | bytes 2654216 | tf_op jit(solution)/shard_map/ppermute | solution.py:1000
  5.7 21.3 %collective-permute-start.3 = (f32[2,48,2304]{2,1,0:T(8,128)}, f32[2,48,2304]{2,1,0:T(8,128)S(1)}, u32[]{:S(2)}, u32[]{:S(2)}) collective-permute-start(f32[2,48,2304]{2,1,0:T(8,128)} %refs_3_.3), channel_id=1, source_target_pairs={{0,2},{1,3},{2,0},{3,1},{4,6},{5,7},{6,4},{7,5},{8,10},{9,11},{10,... | collective-permute-start | bytes 2654216 | tf_op jit(solution)/shard_map/ppermute | solution.py:1008
  9.2 11.6 %collective-permute-start.2 = (f32[1,48,2304]{2,1,0:T(8,128)}, f32[1,48,2304]{2,1,0:T(8,128)S(1)}, u32[]{:S(2)}, u32[]{:S(2)}) collective-permute-start(f32[1,48,2304]{2,1,0:T(8,128)} %get-tuple-element.99), channel_id=1, source_target_pairs={{0,4},{4,0},{8,12},{12,8},{16,20},{20,16},{24,28},{28,24},{1,5},{5... | collective-permute-start | bytes 1327112 | tf_op jit(solution)/shard_map/ppermute | solution.py:1004
  10.7 21.3 %collective-permute-start = (f32[2,48,2304]{2,1,0:T(8,128)}, f32[2,48,2304]{2,1,0:T(8,128)S(1)}, u32[]{:S(2)}, u32[]{:S(2)}) collective-permute-start(f32[2,48,2304]{2,1,0:T(8,128)} %refs_3_.3), channel_id=1, source_target_pairs={{0,1},{1,0},{2,3},{3,2},{4,5},{5,4},{6,7},{7,6},{8,9},{9,8},{10,11... | collective-permute-start | bytes 2654216 | tf_op jit(solution)/shard_map/ppermute | solution.py:1008
  13.0 1.0 copy-start.2
  14.0 0.9 copy-start.3
  27.0 5.0 %collective-permute-start.4 = (f32[2,48,2304]{2,1,0:T(8,128)S(1)}, f32[2,48,2304]{2,1,0:T(8,128)S(1)}, u32[]{:S(2)}, u32[]{:S(2)}) collective-permute-start(f32[2,48,2304]{2,1,0:T(8,128)S(1)} %collective-permute-done.3.refs_2_.refs_5_), channel_id=1, source_target_pairs={{0,1},{1,0},{2,3},{3,2},{4,5},{5,4},{6,7},{7,6},{8,9},{9,8},{10,11... | collective-permute-start | bytes 2654216 | tf_op jit(solution)/shard_map/ppermute | solution.py:1008
  27.1 14.6 %collective-permute-start.5 = (f32[1,48,2304]{2,1,0:T(8,128)S(1)}, f32[1,48,2304]{2,1,0:T(8,128)S(1)}, u32[]{:S(2)}, u32[]{:S(2)}) collective-permute-start(f32[1,48,2304]{2,1,0:T(8,128)S(1)} %collective-permute-done.2.refs_7_), channel_id=1, source_target_pairs={{4,28},{12,4},{20,12},{28,20},{5,29},{13,5},{21,13},{29,21},{6,30}... | collective-permute-start | bytes 1327112 | tf_op jit(solution)/shard_map/ppermute | solution.py:1000
  27.7 15.4 %collective-permute-start.6 = (f32[1,48,2304]{2,1,0:T(8,128)S(1)}, f32[1,48,2304]{2,1,0:T(8,128)S(1)}, u32[]{:S(2)}, u32[]{:S(2)}) collective-permute-start(f32[1,48,2304]{2,1,0:T(8,128)S(1)} %get-tuple-element.63), channel_id=1, source_target_pairs={{0,28},{4,0},{8,4},{12,8},{16,12},{20,16},{24,20},{28,24},{1,29},{... | collective-permute-start | bytes 1327112 | tf_op jit(solution)/shard_map/ppermute | solution.py:1000
  32.0 1.2 %copy-start = (f32[2,48,2304]{2,1,0:T(8,128)S(1)}, f32[2,48,2304]{2,1,0:T(8,128)}, u32[]{:S(2)}) copy-start(f32[2,48,2304]{2,1,0:T(8,128)} %refs_3_.3) | copy-start | bytes 2654212
  43.1 13.6 %collective-permute-start.8 = (f32[1,864,128]{2,1,0:T(8,128)S(1)}, f32[1,864,128]{2,1,0:T(8,128)S(1)}, u32[]{:S(2)}, u32[]{:S(2)}) collective-permute-start(f32[1,864,128]{2,1,0:T(8,128)S(1)} %get-tuple-element.72), channel_id=1, source_target_pairs={{0,8},{4,12},{8,16},{12,20},{16,24},{20,28},{24,0},{28,4},{1,9},{5... | collective-permute-start | bytes 1327112 | tf_op jit(solution)/shard_map/ppermute | solution.py:1000
  43.9 31.6 %copy-start.1 = (f32[2,48,2304]{2,1,0:T(8,128)S(1)}, f32[2,48,2304]{2,1,0:T(8,128)}, u32[]{:S(2)}) copy-start(f32[2,48,2304]{2,1,0:T(8,128)} %refs_3_.3) | copy-start | bytes 2654212
  56.7 2.6 %collective-permute-start.9 = (f32[8,216,128]{2,1,0:T(8,128)S(1)}, f32[8,216,128]{2,1,0:T(8,128)S(1)}, u32[]{:S(2)}, u32[]{:S(2)}) collective-permute-start(f32[8,216,128]{2,1,0:T(8,128)S(1)} %get-tuple-element.74), channel_id=1, source_target_pairs={{0,1},{1,0},{2,3},{3,2},{4,5},{5,4},{6,7},{7,6},{8,9},{9,8},{10,11... | collective-permute-start | bytes 2654216 | tf_op jit(solution)/shard_map/ppermute | solution.py:1008
  56.7 13.2 %collective-permute-start.11 = (f32[1,864,128]{2,1,0:T(8,128)S(1)}, f32[1,864,128]{2,1,0:T(8,128)S(1)}, u32[]{:S(2)}, u32[]{:S(2)}) collective-permute-start(f32[1,864,128]{2,1,0:T(8,128)S(1)} %get-tuple-element.78), channel_id=1, source_target_pairs={{0,4},{4,0},{8,12},{12,8},{16,20},{20,16},{24,28},{28,24},{1,5},{5... | collective-permute-start | bytes 1327112 | tf_op jit(solution)/shard_map/ppermute | solution.py:1004
  59.1 18.0 %collective-permute-start.7 = (f32[8,216,128]{2,1,0:T(8,128)S(1)}, f32[8,216,128]{2,1,0:T(8,128)S(1)}, u32[]{:S(2)}, u32[]{:S(2)}) collective-permute-start(f32[8,216,128]{2,1,0:T(8,128)S(1)} %get-tuple-element.69), channel_id=1, source_target_pairs={{0,1},{1,0},{2,3},{3,2},{4,5},{5,4},{6,7},{7,6},{8,9},{9,8},{10,11... | collective-permute-start | bytes 2654216 | tf_op jit(solution)/shard_map/ppermute | solution.py:1008
  59.3 14.2 %collective-permute-start.12 = (f32[1,864,128]{2,1,0:T(8,128)S(1)}, f32[1,864,128]{2,1,0:T(8,128)S(1)}, u32[]{:S(2)}, u32[]{:S(2)}) collective-permute-start(f32[1,864,128]{2,1,0:T(8,128)S(1)} %get-tuple-element.80), channel_id=1, source_target_pairs={{0,8},{4,12},{8,16},{12,20},{16,24},{20,28},{24,0},{28,4},{1,9},{5... | collective-permute-start | bytes 1327112 | tf_op jit(solution)/shard_map/ppermute | solution.py:1000
  59.4 21.9 %collective-permute-start.10 = (f32[8,216,128]{2,1,0:T(8,128)S(1)}, f32[8,216,128]{2,1,0:T(8,128)S(1)}, u32[]{:S(2)}, u32[]{:S(2)}) collective-permute-start(f32[8,216,128]{2,1,0:T(8,128)S(1)} %add.3), channel_id=1, source_target_pairs={{0,2},{1,3},{2,0},{3,1},{4,6},{5,7},{6,4},{7,5},{8,10},{9,11},{10,... | collective-permute-start | bytes 2654216 | tf_op jit(solution)/shard_map/ppermute | solution.py:1008
  73.4 15.2 %collective-permute-start.13 = (f32[1,864,128]{2,1,0:T(8,128)S(1)}, f32[1,864,128]{2,1,0:T(8,128)S(1)}, u32[]{:S(2)}, u32[]{:S(2)}) collective-permute-start(f32[1,864,128]{2,1,0:T(8,128)S(1)} %collective-permute-done.11.refs_1_), channel_id=1, source_target_pairs={{0,8},{8,16},{16,24},{24,0},{1,9},{9,17},{17,25},{25,1},{2,10},{10... | collective-permute-start | bytes 1327112 | tf_op jit(solution)/shard_map/ppermute | solution.py:1000
  75.4 14.3 %collective-permute-start.18 = (f32[1,864,128]{2,1,0:T(8,128)S(1)}, f32[1,864,128]{2,1,0:T(8,128)S(1)}, u32[]{:S(2)}, u32[]{:S(2)}) collective-permute-start(f32[1,864,128]{2,1,0:T(8,128)S(1)} %get-tuple-element.90), channel_id=1, source_target_pairs={{0,4},{4,8},{8,12},{12,16},{16,20},{20,24},{24,28},{28,0},{1,5},{5... | collective-permute-start | bytes 1327112 | tf_op jit(solution)/shard_map/ppermute | solution.py:1000
  90.7 4.9 %collective-permute-start.21 = (f32[224,128]{1,0:T(8,128)S(1)}, f32[224,128]{1,0:T(8,128)S(1)}, u32[]{:S(2)}, u32[]{:S(2)}) collective-permute-start(f32[224,128]{1,0:T(8,128)S(1)} %get-tuple-element.95), channel_id=1, source_target_pairs={{0,2},{1,3},{2,0},{3,1},{4,6},{5,7},{6,4},{7,5},{8,10},{9,11},{10,... | collective-permute-start | bytes 344072 | tf_op jit(solution)/shard_map/ppermute | solution.py:1008
  92.3 4.8 %collective-permute-start.19 = (f32[224,128]{1,0:T(8,128)S(1)}, f32[224,128]{1,0:T(8,128)S(1)}, u32[]{:S(2)}, u32[]{:S(2)}) collective-permute-start(f32[224,128]{1,0:T(8,128)S(1)} %get-tuple-element.93), channel_id=1, source_target_pairs={{0,1},{1,0},{2,3},{3,2},{4,5},{5,4},{6,7},{7,6},{8,9},{9,8},{10,11... | collective-permute-start | bytes 344072 | tf_op jit(solution)/shard_map/ppermute | solution.py:1008
  93.4 6.0 %collective-permute-start.16 = (f32[224,128]{1,0:T(8,128)S(1)}, f32[224,128]{1,0:T(8,128)S(1)}, u32[]{:S(2)}, u32[]{:S(2)}) collective-permute-start(f32[224,128]{1,0:T(8,128)S(1)} %get-tuple-element.88), channel_id=1, source_target_pairs={{0,2},{1,3},{2,0},{3,1},{4,6},{5,7},{6,4},{7,5},{8,10},{9,11},{10,... | collective-permute-start | bytes 344072 | tf_op jit(solution)/shard_map/ppermute | solution.py:1008
  94.0 7.9 %collective-permute-start.20 = (f32[224,128]{1,0:T(8,128)S(1)}, f32[224,128]{1,0:T(8,128)S(1)}, u32[]{:S(2)}, u32[]{:S(2)}) collective-permute-start(f32[224,128]{1,0:T(8,128)S(1)} %get-tuple-element.94), channel_id=1, source_target_pairs={{0,2},{1,3},{2,0},{3,1},{4,6},{5,7},{6,4},{7,5},{8,10},{9,11},{10,... | collective-permute-start | bytes 344072 | tf_op jit(solution)/shard_map/ppermute | solution.py:1008
  95.5 6.4 %collective-permute-start.14 = (f32[224,128]{1,0:T(8,128)S(1)}, f32[224,128]{1,0:T(8,128)S(1)}, u32[]{:S(2)}, u32[]{:S(2)}) collective-permute-start(f32[224,128]{1,0:T(8,128)S(1)} %get-tuple-element.86), channel_id=1, source_target_pairs={{0,1},{1,0},{2,3},{3,2},{4,5},{5,4},{6,7},{7,6},{8,9},{9,8},{10,11... | collective-permute-start | bytes 344072 | tf_op jit(solution)/shard_map/ppermute | solution.py:1008
  95.6 8.4 %collective-permute-start.15 = (f32[224,128]{1,0:T(8,128)S(1)}, f32[224,128]{1,0:T(8,128)S(1)}, u32[]{:S(2)}, u32[]{:S(2)}) collective-permute-start(f32[224,128]{1,0:T(8,128)S(1)} %get-tuple-element.87), channel_id=1, source_target_pairs={{0,2},{1,3},{2,0},{3,1},{4,6},{5,7},{6,4},{7,5},{8,10},{9,11},{10,... | collective-permute-start | bytes 344072 | tf_op jit(solution)/shard_map/ppermute | solution.py:1008
  97.1 6.9 %collective-permute-start.22 = (f32[224,128]{1,0:T(8,128)S(1)}, f32[224,128]{1,0:T(8,128)S(1)}, u32[]{:S(2)}, u32[]{:S(2)}) collective-permute-start(f32[224,128]{1,0:T(8,128)S(1)} %collective-permute-done.21), channel_id=1, source_target_pairs={{0,1},{1,0},{2,3},{3,2},{4,5},{5,4},{6,7},{7,6},{8,9},{9,8},{10,11... | collective-permute-start | bytes 344072 | tf_op jit(solution)/shard_map/ppermute | solution.py:1008
  99.4 4.5 %collective-permute-start.17 = (f32[224,128]{1,0:T(8,128)S(1)}, f32[224,128]{1,0:T(8,128)S(1)}, u32[]{:S(2)}, u32[]{:S(2)}) collective-permute-start(f32[224,128]{1,0:T(8,128)S(1)} %collective-permute-done.16), channel_id=1, source_target_pairs={{0,1},{1,0},{2,3},{3,2},{4,5},{5,4},{6,7},{7,6},{8,9},{9,8},{10,11... | collective-permute-start | bytes 344072 | tf_op jit(solution)/shard_map/ppermute | solution.py:1008
